TPU v7x, 32 devices: a whole 2x2x4 slice. The times are simulated.
32 devices in a mesh: seq: 8 (over z, x), head: 4 (over y, core).
Axes of the slice: x: 2, y: 2, z: 4, core: 2. Of those that a mesh axis runs over, the one named last changes fastest.
Arguments:
- queries: bfloat16 [16384, 8192], P(('seq', 'head')), may hold values from -50 to 50
- keys: bfloat16 [16384, 1024], P(('seq', 'head')), may hold values from -6 to 6
- values: bfloat16 [16384, 1024], P(('seq', 'head')), may hold values from -15 to 15
- pattern: int32 [128, 16], replicated, may hold values from 0 to 126, as said below
- keep: int32 [128, 16], replicated, may hold values from 0 to 1, as said below
Outputs:
- attended: bfloat16 [16384, 8192], P(('seq', 'head'))
Inputs may be any that keep to these rules, and one draw needn't show every extreme that they name: `pattern`: entry b of query block i's list is i - 1 for b = 0; for b >= 1 it is i - 2^b or i - 2^b with its lowest bit flipped; it is 0 wherever i < 2^b. `keep`: 0 wherever i < 2^b.
All inputs are finite; a program needn't handle non-finite values.
Results may differ from a plain program's by a relative error of at most 0.0049.
Values may be sent and summed in bfloat16 or wider, within the bound.
No kernel may reach another device: no remote copies, remote signals or barrier semaphores. Data moves between devices by JAX's collectives and lax.ppermute only.
A program may use at most 128 MiB of HBM per device.

v0:
```python
import functools
import math

import jax
import jax.numpy as jnp
from jax import lax
from jax.experimental import pallas as pl
from jax.experimental.pallas import tpu as pltpu
from jax.sharding import PartitionSpec as P

QUERY_HEADS = 64
KEY_VALUE_HEADS = 8
HEAD_SIZE = 128
BLOCK_TOKENS = 128
GROUP = QUERY_HEADS // KEY_VALUE_HEADS
AXES = ("seq", "head")
CHUNKS = (2, 2, 2, 2)
ROW_HEADS = 2
TILE_SLOTS = 2
STEP_BLOCKS = 2
MASKED = -1e30
SCALE = math.log2(math.e) / math.sqrt(HEAD_SIZE)
LEAST_SUM = 1e-25
GREATEST_SUM = 1e30


def attend_kernel(levels, blocks, parts, sources, place_ref, pattern_ref, keep_ref, q_ref, *refs):
    count = len(sources)
    k_refs, v_refs = refs[:count], refs[count : 2 * count]
    out_ref, token_ref = refs[-2:]
    first = place_ref[0] * blocks

    def pick(source, local):
        local = jnp.clip(local, 0, blocks - 1)
        rows = pl.ds(pl.multiple_of(local * BLOCK_TOKENS, BLOCK_TOKENS), BLOCK_TOKENS)
        return k_refs[source][rows, :], v_refs[source][rows, :]

    def gather(block):
        k_part, v_part = pick(0, block)
        ones = jnp.ones_like(v_part)
        k_parts, v_parts, lives = [k_part], [jnp.concatenate([v_part, ones], 1)], []
        for level in range(levels):
            span = 2**level
            named = pattern_ref[first + block, level]
            if span < blocks:
                local = named - first
                near_k, near_v = pick(0, local)
                far_k, far_v = pick(sources.index(1), local + blocks)
                k_part = jnp.where(local >= 0, near_k, far_k)
                v_part = jnp.where(local >= 0, near_v, far_v)
            else:
                shift = span // blocks
                k_part, v_part = pick(sources.index(shift), named - first + shift * blocks)
            live = keep_ref[first + block, level] > 0
            factor = jnp.where(live, 1.0, 0.0).astype(jnp.bfloat16)
            k_parts.append(k_part * factor)
            v_parts.append(jnp.concatenate([v_part * factor, ones * factor], 1))
            lives.append(live)
        return jnp.concatenate(k_parts, 0), jnp.concatenate(v_parts, 0), lives

    def query_rows(part, heads):
        rows = slice(part * BLOCK_TOKENS, (part + 1) * BLOCK_TOKENS)
        return jnp.concatenate(
            [q_ref[rows, h * HEAD_SIZE : (h + 1) * HEAD_SIZE] for h in heads], 0
        )

    def score(q, k):
        return lax.dot_general(
            q, k, (((1,), (1,)), ((), ())), preferred_element_type=jnp.float32
        )

    def store(part, heads, sums):
        total = sums[:, HEAD_SIZE:]
        inverse = pl.reciprocal(total, approx=True)
        inverse = inverse * (2.0 - total * inverse)
        result = (sums[:, :HEAD_SIZE] * inverse).astype(jnp.bfloat16)
        rows = slice(part * BLOCK_TOKENS, (part + 1) * BLOCK_TOKENS)
        for at, h in enumerate(heads):
            out_ref[rows, h * HEAD_SIZE : (h + 1) * HEAD_SIZE] = result[
                at * BLOCK_TOKENS : (at + 1) * BLOCK_TOKENS
            ]

    def causal_of(heads):
        shape = (heads * BLOCK_TOKENS, BLOCK_TOKENS)
        token = lax.broadcasted_iota(jnp.int32, shape, 0) % BLOCK_TOKENS
        return token >= lax.broadcasted_iota(jnp.int32, shape, 1)

    here = pl.program_id(1) * parts

    def quick():
        gathered = [gather(here + part) for part in range(parts)]
        steps = [
            (part, range(h, h + ROW_HEADS))
            for part in range(parts)
            for h in range(0, GROUP, ROW_HEADS)
        ]
        causal = causal_of(ROW_HEADS)

        count_of = levels + 1
        tiles = [
            slice(t * BLOCK_TOKENS, min(t + TILE_SLOTS, count_of) * BLOCK_TOKENS)
            for t in range(0, count_of, TILE_SLOTS)
        ]
        least = jnp.full((8, HEAD_SIZE), GREATEST_SUM, jnp.float32)
        greatest = jnp.full((8, HEAD_SIZE), LEAST_SUM, jnp.float32)
        pieces = [(part, heads, t) for part, heads in steps for t in range(len(tiles))]

        def scores_of(piece):
            part, heads, t = piece
            return score(query_rows(part, heads), gathered[part][0][tiles[t]])

        def weights_of(piece, scores):
            weights = jnp.exp2(scores * SCALE)
            if piece[2] == 0:
                diag = jnp.where(causal, weights[:, :BLOCK_TOKENS], 0.0)
                weights = jnp.concatenate([diag, weights[:, BLOCK_TOKENS:]], 1)
            return weights.astype(jnp.bfloat16)

        def product_of(piece, weights):
            part, _, t = piece
            return jnp.dot(weights, gathered[part][1][tiles[t]], preferred_element_type=jnp.float32)

        ahead = [scores_of(piece) for piece in pieces[:2]]
        behind, sums = None, None
        for at in range(len(pieces) + 1):
            if at + 2 < len(pieces):
                ahead.append(scores_of(pieces[at + 2]))
            weights = None
            if at < len(pieces):
                weights = weights_of(pieces[at], ahead.pop(0))
            if behind is not None:
                part, heads, t = pieces[at - 1]
                product = product_of(pieces[at - 1], behind)
                sums = product if t == 0 else sums + product
                if t == len(tiles) - 1:
                    store(part, heads, sums)
                    total = sums[:, HEAD_SIZE:].reshape(-1, 8, HEAD_SIZE)
                    least = jnp.minimum(least, jnp.min(total, axis=0))
                    greatest = jnp.maximum(greatest, jnp.max(total, axis=0))
            behind = weights
        return least, greatest

    def careful():
        for part in range(parts):
            k, v, lives = gather(here + part)
            bias = jnp.concatenate(
                [
                    jnp.full((1, BLOCK_TOKENS), jnp.where(live, 0.0, MASKED), jnp.float32)
                    for live in lives
                ],
                1,
            )
            causal = causal_of(1)
            for h in range(GROUP):
                scores = score(query_rows(part, [h]), k)
                diag = jnp.where(causal, scores[:, :BLOCK_TOKENS], MASKED)
                scores = jnp.concatenate([diag, scores[:, BLOCK_TOKENS:] + bias], 1)
                peak = jnp.max(scores, axis=1, keepdims=True)
                weights = jnp.exp2((scores - peak) * SCALE).astype(jnp.bfloat16)
                store(part, [h], jnp.dot(weights, v, preferred_element_type=jnp.float32))

    token_ref[0] = 0
    least, greatest = quick()
    fine = (jnp.min(least) > LEAST_SUM) & (jnp.max(greatest) < GREATEST_SUM)
    pl.when(jnp.logical_not(fine))(careful)


def attend_chunk(queries, held, sources, place, pattern, keep, first_head, heads, total, out, waited):
    rows, width = queries.shape
    blocks = rows // BLOCK_TOKENS
    levels = (blocks * total - 1).bit_length()
    group_width = GROUP * HEAD_SIZE

    parts = math.gcd(blocks, STEP_BLOCKS)
    q_block = (parts * BLOCK_TOKENS, group_width)

    def q_index(head, step, *_):
        return step, first_head + head

    in_specs = [pl.BlockSpec(q_block, q_index)]
    operands = [queries]
    for offset in (0, heads):
        for source in sources:
            array, column = held[source]
            in_specs.append(
                pl.BlockSpec(
                    (rows, HEAD_SIZE), lambda head, step, *_, o=column + offset: (0, o + head)
                )
            )
            operands.append(array)
    for array in waited:
        in_specs.append(pl.BlockSpec(memory_space=pl.ANY))
        operands.append(array)
    aliases = {}
    if out is not None:
        in_specs.append(pl.BlockSpec(memory_space=pl.ANY))
        aliases = {3 + len(operands): 0}
        operands.append(out)
    return pl.pallas_call(
        functools.partial(attend_kernel, levels, blocks, parts, sources),
        grid_spec=pltpu.PrefetchScalarGridSpec(
            num_scalar_prefetch=3,
            grid=(heads, blocks // parts),
            in_specs=in_specs,
            out_specs=[
                pl.BlockSpec(q_block, q_index),
                pl.BlockSpec(memory_space=pltpu.SMEM),
            ],
        ),
        out_shape=[
            jax.ShapeDtypeStruct((rows, width), jnp.bfloat16),
            jax.ShapeDtypeStruct((1,), jnp.int32),
        ],
        input_output_aliases=aliases,
        compiler_params=pltpu.CompilerParams(vmem_limit_bytes=44 * 2**20),
        cost_estimate=pl.CostEstimate(
            flops=5000000000,
            bytes_accessed=1,
            transcendentals=1,
        ),
    )(place, pattern, keep, *operands)


def body(queries, keys, values, pattern, keep):
    total = lax.axis_size(AXES)
    place = lax.axis_index(AXES).astype(jnp.int32)
    sources = tuple([0] + [2**b for b in range(total.bit_length() - 1)])
    stride = max(total // 4, 1)
    up = [(p, p + stride) for p in range(total - stride)]
    chunks = range(len(CHUNKS))
    distances = [stride >> k for k in range(1, stride.bit_length() - 1)]
    nearest = distances[-1]
    firsts = [sum(CHUNKS[:c]) for c in chunks]
    held = []
    for first, heads in zip(firsts, CHUNKS):
        columns = slice(first * HEAD_SIZE, (first + heads) * HEAD_SIZE)
        kv = jnp.concatenate([keys[:, columns], values[:, columns]], 1)
        held.append({0: (lax.optimization_barrier(kv), 0)})

    def part_of(chunk, source):
        array, column = held[chunk][source]
        width = 2 * CHUNKS[chunk] * HEAD_SIZE
        return array[:, column * HEAD_SIZE : column * HEAD_SIZE + width]

    def climb(*moves):
        sent = jnp.concatenate([part_of(*move) for move in moves], 1)
        arrived, column = lax.ppermute(sent, AXES, up), 0
        for chunk, source in moves:
            held[chunk][source + stride] = arrived, column
            column += 2 * CHUNKS[chunk]

    def swap(chunk, distance, token=None, other=None):
        upper = (place & distance) > (0 if token is None else token[0])
        sent = jnp.where(upper, part_of(chunk, 2 * distance), part_of(chunk, 0))
        if other is not None:
            sent = jnp.where(other != other, other, sent)
        pairs = [(p, p ^ distance) for p in range(total)]
        held[chunk][distance] = lax.ppermute(sent, AXES, pairs), 0
        if distance == 2:
            sent = jnp.where((place & 1) > 0, sent, part_of(chunk, 0))
            pairs = [(p, p ^ (3 if p & 1 else 1)) for p in range(total)]
            held[chunk][1] = lax.ppermute(sent, AXES, pairs), 0

    state = [None, None]

    def attend(chunk, *waited):
        state[:] = attend_chunk(
            queries,
            held[chunk],
            sources,
            place.reshape(1),
            pattern,
            keep,
            firsts[chunk],
            CHUNKS[chunk],
            total,
            state[0],
            waited,
        )

    climb((0, 0))
    climb((1, 0))
    climb((2, 0), (0, stride))
    climb((3, 0), (1, stride))
    climb((2, stride))
    climb((3, stride))
    for chunk in (0, 1):
        for distance in distances:
            swap(chunk, distance)
    attend(0)
    token = state[1]
    for distance in distances:
        swap(2, distance, token if distance == nearest else None)
    attend(1)
    for distance in distances:
        if distance == distances[0]:
            swap(3, distance, token)
        else:
            swap(3, distance, state[1], part_of(2, 2 * stride))
    attend(2)
    attend(3)
    return state[0]


def solution(mesh):
    return jax.shard_map(
        body,
        mesh=mesh,
        in_specs=(P(AXES, None), P(AXES, None), P(AXES, None), P(), P()),
        out_specs=P(AXES, None),
        check_vma=False,
    )
```

profile of v0, /device:TPU:9, one launch (start us, length us, event | category | flops | bytes accessed | tf_op | source)
XLA Modules:
  0.0 180.3 jit_solution(13341945329707282271)
XLA Ops:
  0.0 2.4 %fusion.1 = (bf16[512,256]{1,0:T(8,128)(2,1)S(1)}, bf16[512,256]{1,0:T(8,128)(2,1)S(1)}, bf16[512,256]{1,0:T(8,128)(2,1)S(1)}, bf16[512,256]{1,0:T(8,128)(2,1)S(...) fusion(bf16[512,1024]{1,0:T(8,128)(2,1)} %param.6, ...), kind=kLoop, calls=%fused_computation.19 | loop fusion | bytes 4194304 | tf_op jit(solution)/shard_map/slice | solution.py:237
  2.4 3.2 %collective-permute-start = (bf16[512,512]{1,0:T(8,128)(2,1)S(1)}, bf16[512,512]{1,0:T(8,128)(2,1)S(1)}, u32[]{:S(2)}, u32[]{:S(2)}) collective-permute-start(bf16[512,512]{1,0:T(8,128)(2,1)S(1)} %pad_maximum_fusion.4.refs_0_.refs_6_), channel_id=1, source_target_pairs={{0,8},{1,9},{2,10},{3,11},{4,12},{5,13},{6,14},{7,15},{8,16},{9,17... | collective-permute-start | bytes 1572872 | tf_op jit(solution)/shard_map/ppermute | solution.py:247
  5.7 3.2 %collective-permute-start.3 = (bf16[512,512]{1,0:T(8,128)(2,1)S(1)}, bf16[512,512]{1,0:T(8,128)(2,1)S(1)}, u32[]{:S(2)}, u32[]{:S(2)}) collective-permute-start(bf16[512,512]{1,0:T(8,128)(2,1)S(1)} %pad_maximum_fusion.5.refs_0_.refs_6_), channel_id=1, source_target_pairs={{0,8},{1,9},{2,10},{3,11},{4,12},{5,13},{6,14},{7,15},{8,16},{9,17... | collective-permute-start | bytes 1572872 | tf_op jit(solution)/shard_map/ppermute | solution.py:247
  10.1 7.0 %collective-permute-done.refs_4_.refs_10_ = bf16[512,512]{1,0:T(8,128)(2,1)S(1)} collective-permute-done((bf16[512,512]{1,0:T(8,128)(2,1)S(1)}, bf16[512,512]{1,0:T(8,128)(2,1)S(1)}, u32[]{:S(2)}, u32[]{:S(2)}) %collective-permute-start) | collective-permute-done | bytes 524320 | tf_op jit(solution)/shard_map/ppermute | solution.py:247
  17.2 1.3 collective-permute-start.8
  18.6 3.2 %collective-permute-start.1 = (bf16[512,1024]{1,0:T(8,128)(2,1)S(1)}, bf16[512,1024]{1,0:T(8,128)(2,1)S(1)}, u32[]{:S(2)}, u32[]{:S(2)}) collective-permute-start(bf16[512,1024]{1,0:T(8,128)(2,1)S(1)} %pad_maximum_fusion), channel_id=1, source_target_pairs={{0,8},{1,9},{2,10},{3,11},{4,12},{5,13},{6,14},{7,15},{8,16},{9,17... | collective-permute-start | bytes 3145736 | tf_op jit(solution)/shard_map/ppermute | solution.py:247
  21.8 6.5 %collective-permute-done.3.refs_4_.refs_10_ = bf16[512,512]{1,0:T(8,128)(2,1)S(1)} collective-permute-done((bf16[512,512]{1,0:T(8,128)(2,1)S(1)}, bf16[512,512]{1,0:T(8,128)(2,1)S(1)}, u32[]{:S(2)}, u32[]{:S(2)}) %collective-permute-start.3) | collective-permute-done | bytes 524320 | tf_op jit(solution)/shard_map/ppermute | solution.py:247
  28.4 1.3 collective-permute-start.4
  29.7 1.1 pad_maximum_fusion.1
  30.9 3.2 %collective-permute-start.7 = (bf16[512,1024]{1,0:T(8,128)(2,1)}, bf16[512,1024]{1,0:T(8,128)(2,1)S(1)}, u32[]{:S(2)}, u32[]{:S(2)}) collective-permute-start(bf16[512,1024]{1,0:T(8,128)(2,1)} %pad_maximum_fusion.1), channel_id=1, source_target_pairs={{0,8},{1,9},{2,10},{3,11},{4,12},{5,13},{6,14},{7,15},{8,16},{9,17... | collective-permute-start | bytes 3145736 | tf_op jit(solution)/shard_map/ppermute | solution.py:247
  34.2 1.3 collective-permute-start.10
  35.5 3.6 %collective-permute-start.9 = (bf16[512,512]{1,0:T(8,128)(2,1)S(1)}, bf16[512,512]{1,0:T(8,128)(2,1)S(1)}, u32[]{:S(2)}, u32[]{:S(2)}) collective-permute-start(bf16[512,512]{1,0:T(8,128)(2,1)S(1)} %get-tuple-element.23), channel_id=1, source_target_pairs={{0,1},{1,2},{2,3},{3,0},{4,5},{5,6},{6,7},{7,4},{8,9},{9,10},{10,1... | collective-permute-start | bytes 1572872 | tf_op jit(solution)/shard_map/ppermute | solution.py:262
  39.2 1.1 broadcast_select_fusion.10
  40.3 4.7 %collective-permute-start.5 = (bf16[512,512]{1,0:T(8,128)(2,1)}, bf16[512,512]{1,0:T(8,128)(2,1)}, u32[]{:S(2)}, u32[]{:S(2)}) collective-permute-start(bf16[512,512]{1,0:T(8,128)(2,1)} %get-tuple-element.21), channel_id=1, source_target_pairs={{0,1},{1,2},{2,3},{3,0},{4,5},{5,6},{6,7},{7,4},{8,9},{9,10},{10,1... | collective-permute-start | bytes 1572872 | tf_op jit(solution)/shard_map/ppermute | solution.py:262
  45.1 5.7 %collective-permute-done.1.refs_5_.refs_11_.refs_4_.refs_10_ = bf16[512,1024]{1,0:T(8,128)(2,1)S(1)} collective-permute-done((bf16[512,1024]{1,0:T(8,128)(2,1)S(1)}, bf16[512,1024]{1,0:T(8,128)(2,1)S(1)}, u32[]{:S(2)}, u32[]{:S(2)}) %collective-permute-start.1) | collective-permute-done | bytes 1048608 | tf_op jit(solution)/shard_map/ppermute | solution.py:247
  50.8 1.2 collective-permute-start.6
  53.2 1.2 collective-permute-start.15
  54.4 26.5 %shard_map.55 = (bf16[512,8192]{1,0:T(8,128)(2,1)}, s32[1]{0:T(128)}) custom-call(s32[1]{0:T(128)} %bitcast.place_ref, s32[128,16]{1,0:T(8,128)S(1)} %copy.15.pattern_ref, s32[128,16]{1,0:T(8,128)S(1)} %copy.16.keep_ref, bf16[512,8192]{1,0:T(8,128)(2,1)} %q_ref.7, bf16[512,512]{1,0:T(8,128)(2,1)S(1)} %copy-done.3, ...), custom_call_target="tpu_custom_call" | custom-call | flops 5000000000 | bytes 1 | tf_op jit(solution)/shard_map/pallas_call | solution.py:199
  82.1 3.3 %collective-permute-start.2 = (bf16[512,512]{1,0:T(8,128)(2,1)}, bf16[512,512]{1,0:T(8,128)(2,1)}, u32[]{:S(2)}, u32[]{:S(2)}) collective-permute-start(bf16[512,512]{1,0:T(8,128)(2,1)} %get-tuple-element.26), channel_id=1, source_target_pairs={{0,8},{1,9},{2,10},{3,11},{4,12},{5,13},{6,14},{7,15},{8,16},{9,17... | collective-permute-start | bytes 1572872 | tf_op jit(solution)/shard_map/ppermute | solution.py:247
  87.8 5.0 %collective-permute-start.16 = (bf16[512,512]{1,0:T(8,128)(2,1)}, bf16[512,512]{1,0:T(8,128)(2,1)}, u32[]{:S(2)}, u32[]{:S(2)}) collective-permute-start(bf16[512,512]{1,0:T(8,128)(2,1)} %get-tuple-element.17), channel_id=1, source_target_pairs={{0,1},{1,2},{2,3},{3,0},{4,5},{5,6},{6,7},{7,4},{8,9},{9,10},{10,1... | collective-permute-start | bytes 1572872 | tf_op jit(solution)/shard_map/ppermute | solution.py:262
  93.0 26.7 %shard_map.56 = (bf16[512,8192]{1,0:T(8,128)(2,1)}, s32[1]{0:T(128)}) custom-call(s32[1]{0:T(128)} %bitcast.place_ref, s32[128,16]{1,0:T(8,128)S(1)} %copy.15.pattern_ref, s32[128,16]{1,0:T(8,128)S(1)} %copy.16.keep_ref, bf16[512,8192]{1,0:T(8,128)(2,1)} %q_ref.7, ...), custom_call_target="tpu_custom_call", output_to_operand_aliasing={{0}: (16, {})} | custom-call | flops 5000000000 | bytes 1 | tf_op jit(solution)/shard_map/pallas_call | solution.py:199
  120.3 3.2 %collective-permute-start.14 = (bf16[512,512]{1,0:T(8,128)(2,1)}, bf16[512,512]{1,0:T(8,128)(2,1)S(1)}, u32[]{:S(2)}, u32[]{:S(2)}) collective-permute-start(bf16[512,512]{1,0:T(8,128)(2,1)} %get-tuple-element.27), channel_id=1, source_target_pairs={{0,8},{1,9},{2,10},{3,11},{4,12},{5,13},{6,14},{7,15},{8,16},{9,17... | collective-permute-start | bytes 1572872 | tf_op jit(solution)/shard_map/ppermute | solution.py:247
  126.9 26.7 %shard_map.57 = (bf16[512,8192]{1,0:T(8,128)(2,1)}, s32[1]{0:T(128)}) custom-call(s32[1]{0:T(128)} %bitcast.place_ref, s32[128,16]{1,0:T(8,128)S(1)} %copy.15.pattern_ref, s32[128,16]{1,0:T(8,128)S(1)} %copy.16.keep_ref, bf16[512,8192]{1,0:T(8,128)(2,1)} %q_ref.7, ...), custom_call_target="tpu_custom_call", output_to_operand_aliasing={{0}: (16, {})} | custom-call | flops 5000000000 | bytes 1 | tf_op jit(solution)/shard_map/pallas_call | solution.py:199
  153.6 26.7 %shard_map.58 = (bf16[512,8192]{1,0:T(8,128)(2,1)}, s32[1]{0:T(128)}) custom-call(s32[1]{0:T(128)} %bitcast.place_ref, s32[128,16]{1,0:T(8,128)S(1)} %copy.15.pattern_ref, s32[128,16]{1,0:T(8,128)S(1)} %copy.16.keep_ref, bf16[512,8192]{1,0:T(8,128)(2,1)} %q_ref.7, ...), custom_call_target="tpu_custom_call", output_to_operand_aliasing={{0}: (16, {})} | custom-call | flops 5000000000 | bytes 1 | tf_op jit(solution)/shard_map/pallas_call | solution.py:199
  (53 shorter events, 8.8 us)
Async XLA Ops:
  2.4 16.2 %copy-start.2 = (bf16[512,512]{1,0:T(8,128)(2,1)}, bf16[512,512]{1,0:T(8,128)(2,1)S(1)}, u32[]{:S(2)}) copy-start(bf16[512,512]{1,0:T(8,128)(2,1)S(1)} %pad_maximum_fusion.4.refs_0_.refs_6_) | copy-start | bytes 1572868
  2.4 14.7 %collective-permute-start = (bf16[512,512]{1,0:T(8,128)(2,1)S(1)}, bf16[512,512]{1,0:T(8,128)(2,1)S(1)}, u32[]{:S(2)}, u32[]{:S(2)}) collective-permute-start(bf16[512,512]{1,0:T(8,128)(2,1)S(1)} %pad_maximum_fusion.4.refs_0_.refs_6_), channel_id=1, source_target_pairs={{0,8},{1,9},{2,10},{3,11},{4,12},{5,13},{6,14},{7,15},{8,16},{9,17... | collective-permute-start | bytes 1572872 | tf_op jit(solution)/shard_map/ppermute | solution.py:247
  5.7 22.7 %collective-permute-start.3 = (bf16[512,512]{1,0:T(8,128)(2,1)S(1)}, bf16[512,512]{1,0:T(8,128)(2,1)S(1)}, u32[]{:S(2)}, u32[]{:S(2)}) collective-permute-start(bf16[512,512]{1,0:T(8,128)(2,1)S(1)} %pad_maximum_fusion.5.refs_0_.refs_6_), channel_id=1, source_target_pairs={{0,8},{1,9},{2,10},{3,11},{4,12},{5,13},{6,14},{7,15},{8,16},{9,17... | collective-permute-start | bytes 1572872 | tf_op jit(solution)/shard_map/ppermute | solution.py:247
  17.1 11.3 %copy-start.6 = (bf16[512,512]{1,0:T(8,128)(2,1)}, bf16[512,512]{1,0:T(8,128)(2,1)S(1)}, u32[]{:S(2)}) copy-start(bf16[512,512]{1,0:T(8,128)(2,1)S(1)} %collective-permute-done.refs_4_.refs_10_) | copy-start | bytes 1572868
  17.2 16.9 %collective-permute-start.8 = (bf16[512,512]{1,0:T(8,128)(2,1)S(1)}, bf16[512,512]{1,0:T(8,128)(2,1)S(1)}, u32[]{:S(2)}, u32[]{:S(2)}) collective-permute-start(bf16[512,512]{1,0:T(8,128)(2,1)S(1)} %broadcast_select_fusion.3), channel_id=1, source_target_pairs={{0,4},{1,5},{2,6},{3,7},{4,0},{5,1},{6,2},{7,3},{8,12},{9,13},{10,... | collective-permute-start | bytes 1572872 | tf_op jit(solution)/shard_map/ppermute | solution.py:258
  18.6 32.2 %collective-permute-start.1 = (bf16[512,1024]{1,0:T(8,128)(2,1)S(1)}, bf16[512,1024]{1,0:T(8,128)(2,1)S(1)}, u32[]{:S(2)}, u32[]{:S(2)}) collective-permute-start(bf16[512,1024]{1,0:T(8,128)(2,1)S(1)} %pad_maximum_fusion), channel_id=1, source_target_pairs={{0,8},{1,9},{2,10},{3,11},{4,12},{5,13},{6,14},{7,15},{8,16},{9,17... | collective-permute-start | bytes 3145736 | tf_op jit(solution)/shard_map/ppermute | solution.py:247
  21.8 12.3 %copy-start.3 = (bf16[512,512]{1,0:T(8,128)(2,1)S(1)}, bf16[512,512]{1,0:T(8,128)(2,1)}, u32[]{:S(2)}) copy-start(bf16[512,512]{1,0:T(8,128)(2,1)} %copy-done.2) | copy-start | bytes 1572868
  28.4 10.8 %collective-permute-start.4 = (bf16[512,512]{1,0:T(8,128)(2,1)S(1)}, bf16[512,512]{1,0:T(8,128)(2,1)S(1)}, u32[]{:S(2)}, u32[]{:S(2)}) collective-permute-start(bf16[512,512]{1,0:T(8,128)(2,1)S(1)} %broadcast_select_fusion.4), channel_id=1, source_target_pairs={{0,4},{1,5},{2,6},{3,7},{4,0},{5,1},{6,2},{7,3},{8,12},{9,13},{10,... | collective-permute-start | bytes 1572872 | tf_op jit(solution)/shard_map/ppermute | solution.py:258
  30.9 54.5 %collective-permute-start.7 = (bf16[512,1024]{1,0:T(8,128)(2,1)}, bf16[512,1024]{1,0:T(8,128)(2,1)S(1)}, u32[]{:S(2)}, u32[]{:S(2)}) collective-permute-start(bf16[512,1024]{1,0:T(8,128)(2,1)} %pad_maximum_fusion.1), channel_id=1, source_target_pairs={{0,8},{1,9},{2,10},{3,11},{4,12},{5,13},{6,14},{7,15},{8,16},{9,17... | collective-permute-start | bytes 3145736 | tf_op jit(solution)/shard_map/ppermute | solution.py:247
  34.2 19.0 %collective-permute-start.10 = (bf16[512,512]{1,0:T(8,128)(2,1)S(1)}, bf16[512,512]{1,0:T(8,128)(2,1)S(1)}, u32[]{:S(2)}, u32[]{:S(2)}) collective-permute-start(bf16[512,512]{1,0:T(8,128)(2,1)S(1)} %get-tuple-element.24), channel_id=1, source_target_pairs={{0,2},{1,3},{2,0},{3,1},{4,6},{5,7},{6,4},{7,5},{8,10},{9,11},{10,... | collective-permute-start | bytes 1572872 | tf_op jit(solution)/shard_map/ppermute | solution.py:258
  35.5 18.9 %copy-start.7 = (bf16[512,512]{1,0:T(8,128)(2,1)S(1)}, bf16[512,512]{1,0:T(8,128)(2,1)}, u32[]{:S(2)}) copy-start(bf16[512,512]{1,0:T(8,128)(2,1)} %copy-done.6) | copy-start | bytes 1572868
  35.5 18.9 %collective-permute-start.9 = (bf16[512,512]{1,0:T(8,128)(2,1)S(1)}, bf16[512,512]{1,0:T(8,128)(2,1)S(1)}, u32[]{:S(2)}, u32[]{:S(2)}) collective-permute-start(bf16[512,512]{1,0:T(8,128)(2,1)S(1)} %get-tuple-element.23), channel_id=1, source_target_pairs={{0,1},{1,2},{2,3},{3,0},{4,5},{5,6},{6,7},{7,4},{8,9},{9,10},{10,1... | collective-permute-start | bytes 1572872 | tf_op jit(solution)/shard_map/ppermute | solution.py:262
  39.2 13.9 %copy-start.4 = (bf16[512,512]{1,0:T(8,128)(2,1)}, bf16[512,512]{1,0:T(8,128)(2,1)S(1)}, u32[]{:S(2)}) copy-start(bf16[512,512]{1,0:T(8,128)(2,1)S(1)} %collective-permute-done.4.refs_3_.refs_9_) | copy-start | bytes 1572868
  40.3 52.5 %collective-permute-start.5 = (bf16[512,512]{1,0:T(8,128)(2,1)}, bf16[512,512]{1,0:T(8,128)(2,1)}, u32[]{:S(2)}, u32[]{:S(2)}) collective-permute-start(bf16[512,512]{1,0:T(8,128)(2,1)} %get-tuple-element.21), channel_id=1, source_target_pairs={{0,1},{1,2},{2,3},{3,0},{4,5},{5,6},{6,7},{7,4},{8,9},{9,10},{10,1... | collective-permute-start | bytes 1572872 | tf_op jit(solution)/shard_map/ppermute | solution.py:262
  50.8 30.1 %copy-start = (bf16[512,1024]{1,0:T(8,128)(2,1)}, bf16[512,1024]{1,0:T(8,128)(2,1)S(1)}, u32[]{:S(2)}) copy-start(bf16[512,1024]{1,0:T(8,128)(2,1)S(1)} %collective-permute-done.1.refs_5_.refs_11_.refs_4_.refs_10_) | copy-start | bytes 3145732
  50.8 42.2 %collective-permute-start.6 = (bf16[512,512]{1,0:T(8,128)(2,1)}, bf16[512,512]{1,0:T(8,128)(2,1)}, u32[]{:S(2)}, u32[]{:S(2)}) collective-permute-start(bf16[512,512]{1,0:T(8,128)(2,1)} %get-tuple-element.22), channel_id=1, source_target_pairs={{0,2},{1,3},{2,0},{3,1},{4,6},{5,7},{6,4},{7,5},{8,10},{9,11},{10,... | collective-permute-start | bytes 1572872 | tf_op jit(solution)/shard_map/ppermute | solution.py:258
  53.2 33.5 %collective-permute-start.15 = (bf16[512,512]{1,0:T(8,128)(2,1)}, bf16[512,512]{1,0:T(8,128)(2,1)}, u32[]{:S(2)}, u32[]{:S(2)}) collective-permute-start(bf16[512,512]{1,0:T(8,128)(2,1)} %get-tuple-element.25), channel_id=1, source_target_pairs={{0,4},{1,5},{2,6},{3,7},{4,0},{5,1},{6,2},{7,3},{8,12},{9,13},{10,... | collective-permute-start | bytes 1572872 | tf_op jit(solution)/shard_map/ppermute | solution.py:258
  82.1 41.5 %collective-permute-start.2 = (bf16[512,512]{1,0:T(8,128)(2,1)}, bf16[512,512]{1,0:T(8,128)(2,1)}, u32[]{:S(2)}, u32[]{:S(2)}) collective-permute-start(bf16[512,512]{1,0:T(8,128)(2,1)} %get-tuple-element.26), channel_id=1, source_target_pairs={{0,8},{1,9},{2,10},{3,11},{4,12},{5,13},{6,14},{7,15},{8,16},{9,17... | collective-permute-start | bytes 1572872 | tf_op jit(solution)/shard_map/ppermute | solution.py:247
  86.4 37.1 %collective-permute-start.11 = (bf16[512,512]{1,0:T(8,128)(2,1)}, bf16[512,512]{1,0:T(8,128)(2,1)}, u32[]{:S(2)}, u32[]{:S(2)}) collective-permute-start(bf16[512,512]{1,0:T(8,128)(2,1)} %get-tuple-element.28), channel_id=1, source_target_pairs={{0,4},{1,5},{2,6},{3,7},{4,0},{5,1},{6,2},{7,3},{8,12},{9,13},{10,... | collective-permute-start | bytes 1572872 | tf_op jit(solution)/shard_map/ppermute | solution.py:258
  87.8 39.0 %collective-permute-start.16 = (bf16[512,512]{1,0:T(8,128)(2,1)}, bf16[512,512]{1,0:T(8,128)(2,1)}, u32[]{:S(2)}, u32[]{:S(2)}) collective-permute-start(bf16[512,512]{1,0:T(8,128)(2,1)} %get-tuple-element.17), channel_id=1, source_target_pairs={{0,1},{1,2},{2,3},{3,0},{4,5},{5,6},{6,7},{7,4},{8,9},{9,10},{10,1... | collective-permute-start | bytes 1572872 | tf_op jit(solution)/shard_map/ppermute | solution.py:262
  92.8 34.1 %collective-permute-start.17 = (bf16[512,512]{1,0:T(8,128)(2,1)}, bf16[512,512]{1,0:T(8,128)(2,1)}, u32[]{:S(2)}, u32[]{:S(2)}) collective-permute-start(bf16[512,512]{1,0:T(8,128)(2,1)} %get-tuple-element.18), channel_id=1, source_target_pairs={{0,2},{1,3},{2,0},{3,1},{4,6},{5,7},{6,4},{7,5},{8,10},{9,11},{10,... | collective-permute-start | bytes 1572872 | tf_op jit(solution)/shard_map/ppermute | solution.py:258
  120.3 33.3 %collective-permute-start.14 = (bf16[512,512]{1,0:T(8,128)(2,1)}, bf16[512,512]{1,0:T(8,128)(2,1)S(1)}, u32[]{:S(2)}, u32[]{:S(2)}) collective-permute-start(bf16[512,512]{1,0:T(8,128)(2,1)} %get-tuple-element.27), channel_id=1, source_target_pairs={{0,8},{1,9},{2,10},{3,11},{4,12},{5,13},{6,14},{7,15},{8,16},{9,17... | collective-permute-start | bytes 1572872 | tf_op jit(solution)/shard_map/ppermute | solution.py:247
  124.7 28.9 %collective-permute-start.12 = (bf16[512,512]{1,0:T(8,128)(2,1)S(1)}, bf16[512,512]{1,0:T(8,128)(2,1)S(1)}, u32[]{:S(2)}, u32[]{:S(2)}) collective-permute-start(bf16[512,512]{1,0:T(8,128)(2,1)S(1)} %get-tuple-element.19), channel_id=1, source_target_pairs={{0,1},{1,2},{2,3},{3,0},{4,5},{5,6},{6,7},{7,4},{8,9},{9,10},{10,1... | collective-permute-start | bytes 1572872 | tf_op jit(solution)/shard_map/ppermute | solution.py:262
  125.8 27.9 %collective-permute-start.13 = (bf16[512,512]{1,0:T(8,128)(2,1)S(1)}, bf16[512,512]{1,0:T(8,128)(2,1)S(1)}, u32[]{:S(2)}, u32[]{:S(2)}) collective-permute-start(bf16[512,512]{1,0:T(8,128)(2,1)S(1)} %get-tuple-element.20), channel_id=1, source_target_pairs={{0,2},{1,3},{2,0},{3,1},{4,6},{5,7},{6,4},{7,5},{8,10},{9,11},{10,... | collective-permute-start | bytes 1572872 | tf_op jit(solution)/shard_map/ppermute | solution.py:258
  (4 other events, 33.4 us)
where the time goes:
time: 182 us; the launch traced here: 180 us
  Pallas kernels  107 us (59%)
  starting transfers between devices  41.6 us (23%)
  waiting for transfers between devices  19.4 us (11%)
  other arithmetic  8.08 us (4%)
  local copies, waits for them, and re-layouts  2.61 us (1%)
  between operations  2.04 us (1%)
    pallas_call x4, Pallas kernels, attend_chunk(): pl.pallas_call(functools.partial(attend_kernel, levels, blocks, parts, so...  107 us
    ppermute x6, starting transfers between devices, climb(): arrived, column = (lax.ppermute(sent, AXES, up), 0)  19.4 us
    ppermute x6, waiting for transfers between devices, climb(): arrived, column = (lax.ppermute(sent, AXES, up), 0)  19.2 us
    ppermute x4, starting transfers between devices, swap(): held[chunk][1] = (lax.ppermute(sent, AXES, pairs), 0)  14.4 us
    ppermute x8, starting transfers between devices, swap(): held[chunk][distance] = (lax.ppermute(sent, AXES, pairs), 0)  7.87 us
  transfers between devices with their start and end apart: 18, of which 4 were waited for; matrix products, arithmetic and copies ran while one was open for 5% of the time, Pallas kernels for 44%

commit v1 on v0

--- a/solution.py
+++ b/solution.py
@@ -14,7 +14,7 @@
 BLOCK_TOKENS = 128
 GROUP = QUERY_HEADS // KEY_VALUE_HEADS
 AXES = ("seq", "head")
-CHUNKS = (2, 2, 2, 2)
+CHUNKS = (2, 3, 2, 1)
 ROW_HEADS = 2
 TILE_SLOTS = 2
 STEP_BLOCKS = 2
@@ -253,6 +253,7 @@
         upper = (place & distance) > (0 if token is None else token[0])
         sent = jnp.where(upper, part_of(chunk, 2 * distance), part_of(chunk, 0))
         if other is not None:
+            other = other[:, : sent.shape[1]]
             sent = jnp.where(other != other, other, sent)
         pairs = [(p, p ^ distance) for p in range(total)]
         held[chunk][distance] = lax.ppermute(sent, AXES, pairs), 0

time: 182 us -> 192 us (1.055)
  waiting for transfers between devices: 19.4 us -> 27.8 us
  other arithmetic: 8.08 us -> 11.7 us
  starting transfers between devices: 41.6 us -> 38.8 us
    ppermute x6, waiting for transfers between devices: 19.2 us -> 27.8 us  [climb(): arrived, column = (lax.ppermute(sent, AXES, up), 0)]
    select_n x3, other arithmetic: 1.2 us -> 4 us  [swap(): sent = jnp.where(upper, part_of(chunk, 2 * distance), part_of(chunk, 0))]
  transfers between devices with their start and end apart: 18 -> 18, of which waited for: 4 -> 3; matrix products, arithmetic and copies ran while one was open for 5% -> 6% of each run, Pallas kernels for 44% -> 48%
where the time goes in v1:
time: 192 us; the launch traced here: 190 us
  Pallas kernels  107 us (56%)
  starting transfers between devices  38.8 us (20%)
  waiting for transfers between devices  27.8 us (14%)
  other arithmetic  11.7 us (6%)
  local copies, waits for them, and re-layouts  2.29 us (1%)
  between operations  2.23 us (1%)
    pallas_call x4, Pallas kernels, attend_chunk(): pl.pallas_call(functools.partial(attend_kernel, levels, blocks, parts, so...  107 us
    ppermute x6, waiting for transfers between devices, climb(): arrived, column = (lax.ppermute(sent, AXES, up), 0)  27.8 us
    ppermute x6, starting transfers between devices, climb(): arrived, column = (lax.ppermute(sent, AXES, up), 0)  19.5 us
    ppermute x4, starting transfers between devices, swap(): held[chunk][1] = (lax.ppermute(sent, AXES, pairs), 0)  13.2 us
    ppermute x8, starting transfers between devices, swap(): held[chunk][distance] = (lax.ppermute(sent, AXES, pairs), 0)  6.2 us
    select_n x3, other arithmetic, swap(): sent = jnp.where(upper, part_of(chunk, 2 * distance), part_of(chunk, 0))  4 us
  transfers between devices with their start and end apart: 18, of which 3 were waited for; matrix products, arithmetic and copies ran while one was open for 6% of the time, Pallas kernels for 48%

profile of v1, /device:TPU:9, one launch (start us, length us, event | category | flops | bytes accessed | tf_op | source)
XLA Modules:
  0.0 189.7 jit_solution(2435396454819478382)
XLA Ops:
  0.0 2.0 %fusion.1 = (bf16[512,256]{1,0:T(8,128)(2,1)S(1)}, bf16[512,256]{1,0:T(8,128)(2,1)S(1)}, bf16[512,256]{1,0:T(8,128)(2,1)S(1)}, bf16[512,256]{1,0:T(8,128)(2,1)}) fusion(bf16[512,1024]{1,0:T(8,128)(2,1)} %param.6, bf16[512,1024]{1,0:T(8,128)(2,1)} %param.7), kind=kLoop, calls=%fused_computation.19 | loop fusion | bytes 2097152 | tf_op jit(solution)/shard_map/slice | solution.py:237
  2.1 3.3 %collective-permute-start = (bf16[512,512]{1,0:T(8,128)(2,1)S(1)}, bf16[512,512]{1,0:T(8,128)(2,1)S(1)}, u32[]{:S(2)}, u32[]{:S(2)}) collective-permute-start(bf16[512,512]{1,0:T(8,128)(2,1)S(1)} %pad_maximum_fusion.4.refs_0_.refs_6_), channel_id=1, source_target_pairs={{0,8},{1,9},{2,10},{3,11},{4,12},{5,13},{6,14},{7,15},{8,16},{9,17... | collective-permute-start | bytes 1572872 | tf_op jit(solution)/shard_map/ppermute | solution.py:247
  5.6 3.2 %collective-permute-start.3 = (bf16[512,768]{1,0:T(8,128)(2,1)S(1)}, bf16[512,768]{1,0:T(8,128)(2,1)S(1)}, u32[]{:S(2)}, u32[]{:S(2)}) collective-permute-start(bf16[512,768]{1,0:T(8,128)(2,1)S(1)} %pad_maximum_fusion.2.refs_0_.refs_6_), channel_id=1, source_target_pairs={{0,8},{1,9},{2,10},{3,11},{4,12},{5,13},{6,14},{7,15},{8,16},{9,17... | collective-permute-start | bytes 2359304 | tf_op jit(solution)/shard_map/ppermute | solution.py:247
  10.0 6.9 %collective-permute-done.refs_4_.refs_10_ = bf16[512,512]{1,0:T(8,128)(2,1)S(1)} collective-permute-done((bf16[512,512]{1,0:T(8,128)(2,1)S(1)}, bf16[512,512]{1,0:T(8,128)(2,1)S(1)}, u32[]{:S(2)}, u32[]{:S(2)}) %collective-permute-start) | collective-permute-done | bytes 524320 | tf_op jit(solution)/shard_map/ppermute | solution.py:247
  16.9 1.1 pad_maximum_fusion
  18.1 3.3 %collective-permute-start.1 = (bf16[512,1024]{1,0:T(8,128)(2,1)}, bf16[512,1024]{1,0:T(8,128)(2,1)}, u32[]{:S(2)}, u32[]{:S(2)}) collective-permute-start(bf16[512,1024]{1,0:T(8,128)(2,1)} %pad_maximum_fusion), channel_id=1, source_target_pairs={{0,8},{1,9},{2,10},{3,11},{4,12},{5,13},{6,14},{7,15},{8,16},{9,17... | collective-permute-start | bytes 3145736 | tf_op jit(solution)/shard_map/ppermute | solution.py:247
  22.3 1.2 collective-permute-start.8
  23.5 10.4 %collective-permute-done.3.refs_4_.refs_10_ = bf16[512,768]{1,0:T(8,128)(2,1)S(1)} collective-permute-done((bf16[512,768]{1,0:T(8,128)(2,1)S(1)}, bf16[512,768]{1,0:T(8,128)(2,1)S(1)}, u32[]{:S(2)}, u32[]{:S(2)}) %collective-permute-start.3) | collective-permute-done | bytes 786464 | tf_op jit(solution)/shard_map/ppermute | solution.py:247
  34.9 1.2 collective-permute-start.4
  37.3 3.2 %collective-permute-start.7 = (bf16[512,1024]{1,0:T(8,128)(2,1)}, bf16[512,1024]{1,0:T(8,128)(2,1)S(1)}, u32[]{:S(2)}, u32[]{:S(2)}) collective-permute-start(bf16[512,1024]{1,0:T(8,128)(2,1)} %pad_maximum_fusion.1), channel_id=1, source_target_pairs={{0,8},{1,9},{2,10},{3,11},{4,12},{5,13},{6,14},{7,15},{8,16},{9,17... | collective-permute-start | bytes 3145736 | tf_op jit(solution)/shard_map/ppermute | solution.py:247
  40.6 5.4 %collective-permute-start.9 = (bf16[512,512]{1,0:T(8,128)(2,1)S(1)}, bf16[512,512]{1,0:T(8,128)(2,1)S(1)}, u32[]{:S(2)}, u32[]{:S(2)}) collective-permute-start(bf16[512,512]{1,0:T(8,128)(2,1)S(1)} %get-tuple-element.23), channel_id=1, source_target_pairs={{0,1},{1,2},{2,3},{3,0},{4,5},{5,6},{6,7},{7,4},{8,9},{9,10},{10,1... | collective-permute-start | bytes 1572872 | tf_op jit(solution)/shard_map/ppermute | solution.py:263
  45.9 10.4 %collective-permute-done.1.refs_5_.refs_11_.refs_4_.refs_10_ = bf16[512,1024]{1,0:T(8,128)(2,1)} collective-permute-done((bf16[512,1024]{1,0:T(8,128)(2,1)}, bf16[512,1024]{1,0:T(8,128)(2,1)}, u32[]{:S(2)}, u32[]{:S(2)}) %collective-permute-start.1) | collective-permute-done | bytes 1048608 | tf_op jit(solution)/shard_map/ppermute | solution.py:247
  56.4 2.2 %broadcast_select_fusion.4 = (bf16[512,512]{1,0:T(8,128)(2,1)}, bf16[512,512]{1,0:T(8,128)(2,1)}) fusion(bf16[512,512]{1,0:T(8,128)(2,1)S(1)} %pad_maximum_fusion.3.refs_0_.refs_6_, pred[]{:T(512)S(6)} %gt.26, bf16[512,1024]{1,0:T(8,128)(2,1)} %collective-permute-done.1.refs_5_.refs_11_.refs_4_.refs_10_), kind=kLoop, calls=%fused_computation.10 | loop fusion | flops 262144 | bytes 2097153 | tf_op jit(solution)/shard_map/jit(_where)/select_n | solution.py:254
  58.5 1.2 collective-permute-start.15
  59.8 1.3 broadcast_select_fusion.2
  61.1 5.2 %collective-permute-start.5 = (bf16[512,768]{1,0:T(8,128)(2,1)}, bf16[512,768]{1,0:T(8,128)(2,1)}, u32[]{:S(2)}, u32[]{:S(2)}) collective-permute-start(bf16[512,768]{1,0:T(8,128)(2,1)} %get-tuple-element.21), channel_id=1, source_target_pairs={{0,1},{1,2},{2,3},{3,0},{4,5},{5,6},{6,7},{7,4},{8,9},{9,10},{10,1... | collective-permute-start | bytes 2359304 | tf_op jit(solution)/shard_map/ppermute | solution.py:263
  66.3 26.7 %shard_map.55 = (bf16[512,8192]{1,0:T(8,128)(2,1)}, s32[1]{0:T(128)}) custom-call(s32[1]{0:T(128)} %bitcast.place_ref, s32[128,16]{1,0:T(8,128)S(1)} %copy.15.pattern_ref, s32[128,16]{1,0:T(8,128)S(1)} %copy.16.keep_ref, bf16[512,8192]{1,0:T(8,128)(2,1)} %q_ref.7, bf16[512,512]{1,0:T(8,128)(2,1)S(1)} %copy-done.1, ...), custom_call_target="tpu_custom_call" | custom-call | flops 5000000000 | bytes 1 | tf_op jit(solution)/shard_map/pallas_call | solution.py:199
  94.4 3.2 %collective-permute-start.2 = (bf16[512,512]{1,0:T(8,128)(2,1)}, bf16[512,512]{1,0:T(8,128)(2,1)}, u32[]{:S(2)}, u32[]{:S(2)}) collective-permute-start(bf16[512,512]{1,0:T(8,128)(2,1)} %get-tuple-element.26), channel_id=1, source_target_pairs={{0,8},{1,9},{2,10},{3,11},{4,12},{5,13},{6,14},{7,15},{8,16},{9,17... | collective-permute-start | bytes 1572872 | tf_op jit(solution)/shard_map/ppermute | solution.py:247
  98.8 3.2 %collective-permute-start.14 = (bf16[512,256]{1,0:T(8,128)(2,1)}, bf16[512,256]{1,0:T(8,128)(2,1)}, u32[]{:S(2)}, u32[]{:S(2)}) collective-permute-start(bf16[512,256]{1,0:T(8,128)(2,1)} %get-tuple-element.27), channel_id=1, source_target_pairs={{0,8},{1,9},{2,10},{3,11},{4,12},{5,13},{6,14},{7,15},{8,16},{9,17... | collective-permute-start | bytes 786440 | tf_op jit(solution)/shard_map/ppermute | solution.py:247
  103.1 1.9 %collective-permute-start.16 = (bf16[512,512]{1,0:T(8,128)(2,1)}, bf16[512,512]{1,0:T(8,128)(2,1)}, u32[]{:S(2)}, u32[]{:S(2)}) collective-permute-start(bf16[512,512]{1,0:T(8,128)(2,1)} %get-tuple-element.17), channel_id=1, source_target_pairs={{0,1},{1,2},{2,3},{3,0},{4,5},{5,6},{6,7},{7,4},{8,9},{9,10},{10,1... | collective-permute-start | bytes 1572872 | tf_op jit(solution)/shard_map/ppermute | solution.py:263
  105.7 37.8 %shard_map.56 = (bf16[512,8192]{1,0:T(8,128)(2,1)}, s32[1]{0:T(128)}) custom-call(s32[1]{0:T(128)} %bitcast.place_ref, s32[128,16]{1,0:T(8,128)S(1)} %copy.15.pattern_ref, s32[128,16]{1,0:T(8,128)S(1)} %copy.16.keep_ref, bf16[512,8192]{1,0:T(8,128)(2,1)} %q_ref.7, ...), custom_call_target="tpu_custom_call", output_to_operand_aliasing={{0}: (16, {})} | custom-call | flops 5000000000 | bytes 1 | tf_op jit(solution)/shard_map/pallas_call | solution.py:199
  145.8 1.6 collective-permute-start.13
  147.4 26.7 %shard_map.57 = (bf16[512,8192]{1,0:T(8,128)(2,1)}, s32[1]{0:T(128)}) custom-call(s32[1]{0:T(128)} %bitcast.place_ref, s32[128,16]{1,0:T(8,128)S(1)} %copy.15.pattern_ref, s32[128,16]{1,0:T(8,128)S(1)} %copy.16.keep_ref, bf16[512,8192]{1,0:T(8,128)(2,1)} %q_ref.7, ...), custom_call_target="tpu_custom_call", output_to_operand_aliasing={{0}: (16, {})} | custom-call | flops 5000000000 | bytes 1 | tf_op jit(solution)/shard_map/pallas_call | solution.py:199
  174.2 15.5 %shard_map.58 = (bf16[512,8192]{1,0:T(8,128)(2,1)}, s32[1]{0:T(128)}) custom-call(s32[1]{0:T(128)} %bitcast.place_ref, s32[128,16]{1,0:T(8,128)S(1)} %copy.15.pattern_ref, s32[128,16]{1,0:T(8,128)S(1)} %copy.16.keep_ref, bf16[512,8192]{1,0:T(8,128)(2,1)} %q_ref.7, ...), custom_call_target="tpu_custom_call", output_to_operand_aliasing={{0}: (16, {})} | custom-call | flops 5000000000 | bytes 1 | tf_op jit(solution)/shard_map/pallas_call | solution.py:199
  (53 shorter events, 9.0 us)
Async XLA Ops:
  2.1 19.3 %copy-start = (bf16[512,512]{1,0:T(8,128)(2,1)}, bf16[512,512]{1,0:T(8,128)(2,1)S(1)}, u32[]{:S(2)}) copy-start(bf16[512,512]{1,0:T(8,128)(2,1)S(1)} %pad_maximum_fusion.4.refs_0_.refs_6_) | copy-start | bytes 1572868
  2.1 6.8 %copy-start.5 = (s32[128,16]{0,1:T(8,128)S(1)}, s32[128,16]{0,1:T(8,128)}, u32[]{:S(2)}) copy-start(s32[128,16]{0,1:T(8,128)} %param.9) | copy-start | bytes 24580
  2.1 14.8 %collective-permute-start = (bf16[512,512]{1,0:T(8,128)(2,1)S(1)}, bf16[512,512]{1,0:T(8,128)(2,1)S(1)}, u32[]{:S(2)}, u32[]{:S(2)}) collective-permute-start(bf16[512,512]{1,0:T(8,128)(2,1)S(1)} %pad_maximum_fusion.4.refs_0_.refs_6_), channel_id=1, source_target_pairs={{0,8},{1,9},{2,10},{3,11},{4,12},{5,13},{6,14},{7,15},{8,16},{9,17... | collective-permute-start | bytes 1572872 | tf_op jit(solution)/shard_map/ppermute | solution.py:247
  5.6 28.3 %collective-permute-start.3 = (bf16[512,768]{1,0:T(8,128)(2,1)S(1)}, bf16[512,768]{1,0:T(8,128)(2,1)S(1)}, u32[]{:S(2)}, u32[]{:S(2)}) collective-permute-start(bf16[512,768]{1,0:T(8,128)(2,1)S(1)} %pad_maximum_fusion.2.refs_0_.refs_6_), channel_id=1, source_target_pairs={{0,8},{1,9},{2,10},{3,11},{4,12},{5,13},{6,14},{7,15},{8,16},{9,17... | collective-permute-start | bytes 2359304 | tf_op jit(solution)/shard_map/ppermute | solution.py:247
  16.9 17.9 %copy-start.2 = (bf16[512,512]{1,0:T(8,128)(2,1)}, bf16[512,512]{1,0:T(8,128)(2,1)S(1)}, u32[]{:S(2)}) copy-start(bf16[512,512]{1,0:T(8,128)(2,1)S(1)} %collective-permute-done.refs_4_.refs_10_) | copy-start | bytes 1572868
  18.1 18.0 %slice-start.1 = ((bf16[512,1024]{1,0:T(8,128)(2,1)}), bf16[512,128]{1,0:T(8,128)(2,1)S(1)}, s32[]{:S(2)}) async-start(bf16[512,1024]{1,0:T(8,128)(2,1)} %param.7), calls=%async_computation.1 | async-start | bytes 262144 | tf_op jit(solution)/shard_map/slice | solution.py:237
  18.1 18.0 %slice-start.3 = ((bf16[512,1024]{1,0:T(8,128)(2,1)}), bf16[512,128]{1,0:T(8,128)(2,1)S(1)}, s32[]{:S(2)}) async-start(bf16[512,1024]{1,0:T(8,128)(2,1)} %param.6), calls=%async_computation.3 | async-start | bytes 262144 | tf_op jit(solution)/shard_map/slice | solution.py:237
  18.1 38.3 %collective-permute-start.1 = (bf16[512,1024]{1,0:T(8,128)(2,1)}, bf16[512,1024]{1,0:T(8,128)(2,1)}, u32[]{:S(2)}, u32[]{:S(2)}) collective-permute-start(bf16[512,1024]{1,0:T(8,128)(2,1)} %pad_maximum_fusion), channel_id=1, source_target_pairs={{0,8},{1,9},{2,10},{3,11},{4,12},{5,13},{6,14},{7,15},{8,16},{9,17... | collective-permute-start | bytes 3145736 | tf_op jit(solution)/shard_map/ppermute | solution.py:247
  22.3 18.2 %collective-permute-start.8 = (bf16[512,512]{1,0:T(8,128)(2,1)}, bf16[512,512]{1,0:T(8,128)(2,1)}, u32[]{:S(2)}, u32[]{:S(2)}) collective-permute-start(bf16[512,512]{1,0:T(8,128)(2,1)} %broadcast_select_fusion.5), channel_id=1, source_target_pairs={{0,4},{1,5},{2,6},{3,7},{4,0},{5,1},{6,2},{7,3},{8,12},{9,13},{10,... | collective-permute-start | bytes 1572872 | tf_op jit(solution)/shard_map/ppermute | solution.py:259
  34.9 24.9 %collective-permute-start.4 = (bf16[512,768]{1,0:T(8,128)(2,1)}, bf16[512,768]{1,0:T(8,128)(2,1)}, u32[]{:S(2)}, u32[]{:S(2)}) collective-permute-start(bf16[512,768]{1,0:T(8,128)(2,1)} %broadcast_select_fusion), channel_id=1, source_target_pairs={{0,4},{1,5},{2,6},{3,7},{4,0},{5,1},{6,2},{7,3},{8,12},{9,13},{10,... | collective-permute-start | bytes 2359304 | tf_op jit(solution)/shard_map/ppermute | solution.py:259
  37.3 60.4 %collective-permute-start.7 = (bf16[512,1024]{1,0:T(8,128)(2,1)}, bf16[512,1024]{1,0:T(8,128)(2,1)S(1)}, u32[]{:S(2)}, u32[]{:S(2)}) collective-permute-start(bf16[512,1024]{1,0:T(8,128)(2,1)} %pad_maximum_fusion.1), channel_id=1, source_target_pairs={{0,8},{1,9},{2,10},{3,11},{4,12},{5,13},{6,14},{7,15},{8,16},{9,17... | collective-permute-start | bytes 3145736 | tf_op jit(solution)/shard_map/ppermute | solution.py:247
  40.6 25.7 %collective-permute-start.9 = (bf16[512,512]{1,0:T(8,128)(2,1)S(1)}, bf16[512,512]{1,0:T(8,128)(2,1)S(1)}, u32[]{:S(2)}, u32[]{:S(2)}) collective-permute-start(bf16[512,512]{1,0:T(8,128)(2,1)S(1)} %get-tuple-element.23), channel_id=1, source_target_pairs={{0,1},{1,2},{2,3},{3,0},{4,5},{5,6},{6,7},{7,4},{8,9},{9,10},{10,1... | collective-permute-start | bytes 1572872 | tf_op jit(solution)/shard_map/ppermute | solution.py:263
  45.9 20.4 %collective-permute-start.10 = (bf16[512,512]{1,0:T(8,128)(2,1)S(1)}, bf16[512,512]{1,0:T(8,128)(2,1)S(1)}, u32[]{:S(2)}, u32[]{:S(2)}) collective-permute-start(bf16[512,512]{1,0:T(8,128)(2,1)S(1)} %get-tuple-element.24), channel_id=1, source_target_pairs={{0,2},{1,3},{2,0},{3,1},{4,6},{5,7},{6,4},{7,5},{8,10},{9,11},{10,... | collective-permute-start | bytes 1572872 | tf_op jit(solution)/shard_map/ppermute | solution.py:259
  58.5 7.8 %copy-start.3 = (bf16[512,512]{1,0:T(8,128)(2,1)S(1)}, bf16[512,512]{1,0:T(8,128)(2,1)}, u32[]{:S(2)}) copy-start(bf16[512,512]{1,0:T(8,128)(2,1)} %copy-done.2) | copy-start | bytes 1572868
  58.5 40.3 %collective-permute-start.15 = (bf16[512,512]{1,0:T(8,128)(2,1)}, bf16[512,512]{1,0:T(8,128)(2,1)}, u32[]{:S(2)}, u32[]{:S(2)}) collective-permute-start(bf16[512,512]{1,0:T(8,128)(2,1)} %get-tuple-element.25), channel_id=1, source_target_pairs={{0,4},{1,5},{2,6},{3,7},{4,0},{5,1},{6,2},{7,3},{8,12},{9,13},{10,... | collective-permute-start | bytes 1572872 | tf_op jit(solution)/shard_map/ppermute | solution.py:259
  61.1 42.0 %collective-permute-start.5 = (bf16[512,768]{1,0:T(8,128)(2,1)}, bf16[512,768]{1,0:T(8,128)(2,1)}, u32[]{:S(2)}, u32[]{:S(2)}) collective-permute-start(bf16[512,768]{1,0:T(8,128)(2,1)} %get-tuple-element.21), channel_id=1, source_target_pairs={{0,1},{1,2},{2,3},{3,0},{4,5},{5,6},{6,7},{7,4},{8,9},{9,10},{10,1... | collective-permute-start | bytes 2359304 | tf_op jit(solution)/shard_map/ppermute | solution.py:263
  66.3 38.7 %collective-permute-start.6 = (bf16[512,768]{1,0:T(8,128)(2,1)}, bf16[512,768]{1,0:T(8,128)(2,1)}, u32[]{:S(2)}, u32[]{:S(2)}) collective-permute-start(bf16[512,768]{1,0:T(8,128)(2,1)} %get-tuple-element.22), channel_id=1, source_target_pairs={{0,2},{1,3},{2,0},{3,1},{4,6},{5,7},{6,4},{7,5},{8,10},{9,11},{10,... | collective-permute-start | bytes 2359304 | tf_op jit(solution)/shard_map/ppermute | solution.py:259
  94.4 49.6 %collective-permute-start.2 = (bf16[512,512]{1,0:T(8,128)(2,1)}, bf16[512,512]{1,0:T(8,128)(2,1)}, u32[]{:S(2)}, u32[]{:S(2)}) collective-permute-start(bf16[512,512]{1,0:T(8,128)(2,1)} %get-tuple-element.26), channel_id=1, source_target_pairs={{0,8},{1,9},{2,10},{3,11},{4,12},{5,13},{6,14},{7,15},{8,16},{9,17... | collective-permute-start | bytes 1572872 | tf_op jit(solution)/shard_map/ppermute | solution.py:247
  98.6 45.5 %collective-permute-start.11 = (bf16[512,256]{1,0:T(8,128)(2,1)}, bf16[512,256]{1,0:T(8,128)(2,1)}, u32[]{:S(2)}, u32[]{:S(2)}) collective-permute-start(bf16[512,256]{1,0:T(8,128)(2,1)} %get-tuple-element.28), channel_id=1, source_target_pairs={{0,4},{1,5},{2,6},{3,7},{4,0},{5,1},{6,2},{7,3},{8,12},{9,13},{10,... | collective-permute-start | bytes 786440 | tf_op jit(solution)/shard_map/ppermute | solution.py:259
  98.8 75.3 %collective-permute-start.14 = (bf16[512,256]{1,0:T(8,128)(2,1)}, bf16[512,256]{1,0:T(8,128)(2,1)}, u32[]{:S(2)}, u32[]{:S(2)}) collective-permute-start(bf16[512,256]{1,0:T(8,128)(2,1)} %get-tuple-element.27), channel_id=1, source_target_pairs={{0,8},{1,9},{2,10},{3,11},{4,12},{5,13},{6,14},{7,15},{8,16},{9,17... | collective-permute-start | bytes 786440 | tf_op jit(solution)/shard_map/ppermute | solution.py:247
  103.1 44.3 %collective-permute-start.16 = (bf16[512,512]{1,0:T(8,128)(2,1)}, bf16[512,512]{1,0:T(8,128)(2,1)}, u32[]{:S(2)}, u32[]{:S(2)}) collective-permute-start(bf16[512,512]{1,0:T(8,128)(2,1)} %get-tuple-element.17), channel_id=1, source_target_pairs={{0,1},{1,2},{2,3},{3,0},{4,5},{5,6},{6,7},{7,4},{8,9},{9,10},{10,1... | collective-permute-start | bytes 1572872 | tf_op jit(solution)/shard_map/ppermute | solution.py:263
  105.0 42.4 %collective-permute-start.17 = (bf16[512,512]{1,0:T(8,128)(2,1)}, bf16[512,512]{1,0:T(8,128)(2,1)}, u32[]{:S(2)}, u32[]{:S(2)}) collective-permute-start(bf16[512,512]{1,0:T(8,128)(2,1)} %get-tuple-element.18), channel_id=1, source_target_pairs={{0,2},{1,3},{2,0},{3,1},{4,6},{5,7},{6,4},{7,5},{8,10},{9,11},{10,... | collective-permute-start | bytes 1572872 | tf_op jit(solution)/shard_map/ppermute | solution.py:259
  145.1 29.0 %collective-permute-start.12 = (bf16[512,256]{1,0:T(8,128)(2,1)S(1)}, bf16[512,256]{1,0:T(8,128)(2,1)S(1)}, u32[]{:S(2)}, u32[]{:S(2)}) collective-permute-start(bf16[512,256]{1,0:T(8,128)(2,1)S(1)} %get-tuple-element.19), channel_id=1, source_target_pairs={{0,1},{1,2},{2,3},{3,0},{4,5},{5,6},{6,7},{7,4},{8,9},{9,10},{10,1... | collective-permute-start | bytes 786440 | tf_op jit(solution)/shard_map/ppermute | solution.py:263
  145.8 28.4 %collective-permute-start.13 = (bf16[512,256]{1,0:T(8,128)(2,1)S(1)}, bf16[512,256]{1,0:T(8,128)(2,1)S(1)}, u32[]{:S(2)}, u32[]{:S(2)}) collective-permute-start(bf16[512,256]{1,0:T(8,128)(2,1)S(1)} %get-tuple-element.20), channel_id=1, source_target_pairs={{0,2},{1,3},{2,0},{3,1},{4,6},{5,7},{6,4},{7,5},{8,10},{9,11},{10,... | collective-permute-start | bytes 786440 | tf_op jit(solution)/shard_map/ppermute | solution.py:259
  (4 other events, 22.0 us)

commit v2 on v0

--- a/solution.py
+++ b/solution.py
@@ -24,7 +24,7 @@
 GREATEST_SUM = 1e30
 
 
-def attend_kernel(levels, blocks, parts, sources, place_ref, pattern_ref, keep_ref, q_ref, *refs):
+def attend_kernel(levels, blocks, parts, sources, place_ref, table_ref, q_ref, *refs):
     count = len(sources)
     k_refs, v_refs = refs[:count], refs[count : 2 * count]
     out_ref, token_ref = refs[-2:]
@@ -41,7 +41,7 @@
         k_parts, v_parts, lives = [k_part], [jnp.concatenate([v_part, ones], 1)], []
         for level in range(levels):
             span = 2**level
-            named = pattern_ref[first + block, level]
+            named = table_ref[block * levels + level]
             if span < blocks:
                 local = named - first
                 near_k, near_v = pick(0, local)
@@ -51,7 +51,7 @@
             else:
                 shift = span // blocks
                 k_part, v_part = pick(sources.index(shift), named - first + shift * blocks)
-            live = keep_ref[first + block, level] > 0
+            live = table_ref[(blocks + block) * levels + level] > 0
             factor = jnp.where(live, 1.0, 0.0).astype(jnp.bfloat16)
             k_parts.append(k_part * factor)
             v_parts.append(jnp.concatenate([v_part * factor, ones * factor], 1))
@@ -165,7 +165,7 @@
     pl.when(jnp.logical_not(fine))(careful)
 
 
-def attend_chunk(queries, held, sources, place, pattern, keep, first_head, heads, total, out, waited):
+def attend_chunk(queries, held, sources, place, table, first_head, heads, total, out, waited):
     rows, width = queries.shape
     blocks = rows // BLOCK_TOKENS
     levels = (blocks * total - 1).bit_length()
@@ -194,12 +194,12 @@
     aliases = {}
     if out is not None:
         in_specs.append(pl.BlockSpec(memory_space=pl.ANY))
-        aliases = {3 + len(operands): 0}
+        aliases = {2 + len(operands): 0}
         operands.append(out)
     return pl.pallas_call(
         functools.partial(attend_kernel, levels, blocks, parts, sources),
         grid_spec=pltpu.PrefetchScalarGridSpec(
-            num_scalar_prefetch=3,
+            num_scalar_prefetch=2,
             grid=(heads, blocks // parts),
             in_specs=in_specs,
             out_specs=[
@@ -218,12 +218,20 @@
             bytes_accessed=1,
             transcendentals=1,
         ),
-    )(place, pattern, keep, *operands)
+    )(place, table, *operands)
 
 
 def body(queries, keys, values, pattern, keep):
     total = lax.axis_size(AXES)
     place = lax.axis_index(AXES).astype(jnp.int32)
+    blocks = queries.shape[0] // BLOCK_TOKENS
+    levels = (blocks * total - 1).bit_length()
+    table = jnp.concatenate(
+        [
+            lax.dynamic_slice_in_dim(x, place * blocks, blocks, 0)[:, :levels].reshape(-1)
+            for x in (pattern, keep)
+        ]
+    )
     sources = tuple([0] + [2**b for b in range(total.bit_length() - 1)])
     stride = max(total // 4, 1)
     up = [(p, p + stride) for p in range(total - stride)]
@@ -269,8 +277,7 @@
             held[chunk],
             sources,
             place.reshape(1),
-            pattern,
-            keep,
+            table,
             firsts[chunk],
             CHUNKS[chunk],
             total,

time: 182 us -> 174 us (0.956)
  Pallas kernels: 107 us -> 98 us
    pallas_call x4, Pallas kernels: 107 us -> 98 us  [attend_chunk(): pl.pallas_call(functools.partial(attend_kernel, levels, blocks, parts, so...]
  transfers between devices with their start and end apart: 18 -> 18, of which waited for: 4 -> 4; matrix products, arithmetic and copies ran while one was open for 5% -> 5% of each run, Pallas kernels for 44% -> 43%
where the time goes in v2:
time: 174 us; the launch traced here: 172 us
  Pallas kernels  98 us (56%)
  starting transfers between devices  41.8 us (24%)
  waiting for transfers between devices  18.9 us (11%)
  other arithmetic  8.19 us (5%)
  local copies, waits for them, and re-layouts  2.84 us (2%)
  between operations  2.11 us (1%)
    pallas_call x4, Pallas kernels, attend_chunk(): pl.pallas_call(functools.partial(attend_kernel, levels, blocks, parts, so...  98 us
    ppermute x6, starting transfers between devices, climb(): arrived, column = (lax.ppermute(sent, AXES, up), 0)  19.5 us
    ppermute x6, waiting for transfers between devices, climb(): arrived, column = (lax.ppermute(sent, AXES, up), 0)  18.8 us
    ppermute x4, starting transfers between devices, swap(): held[chunk][1] = (lax.ppermute(sent, AXES, pairs), 0)  14.4 us
    ppermute x8, starting transfers between devices, swap(): held[chunk][distance] = (lax.ppermute(sent, AXES, pairs), 0)  7.9 us
    select_n x4, other arithmetic, swap(): sent = jnp.where(place & 1 > 0, sent, part_of(chunk, 0))  3.52 us
  transfers between devices with their start and end apart: 18, of which 4 were waited for; matrix products, arithmetic and copies ran while one was open for 5% of the time, Pallas kernels for 43%

profile of v2, /device:TPU:9, one launch (start us, length us, event | category | flops | bytes accessed | tf_op | source)
XLA Modules:
  0.0 171.9 jit_solution(9779814759426140272)
XLA Ops:
  0.0 2.4 %fusion.1 = (bf16[512,256]{1,0:T(8,128)(2,1)S(1)}, bf16[512,256]{1,0:T(8,128)(2,1)S(1)}, bf16[512,256]{1,0:T(8,128)(2,1)S(1)}, bf16[512,256]{1,0:T(8,128)(2,1)S(...) fusion(bf16[512,1024]{1,0:T(8,128)(2,1)} %param.6, ...), kind=kLoop, calls=%fused_computation.22 | loop fusion | bytes 4194304 | tf_op jit(solution)/shard_map/slice | solution.py:245
  2.4 3.2 %collective-permute-start = (bf16[512,512]{1,0:T(8,128)(2,1)S(1)}, bf16[512,512]{1,0:T(8,128)(2,1)S(1)}, u32[]{:S(2)}, u32[]{:S(2)}) collective-permute-start(bf16[512,512]{1,0:T(8,128)(2,1)S(1)} %pad_maximum_fusion.4.refs_0_.refs_6_), channel_id=1, source_target_pairs={{0,8},{1,9},{2,10},{3,11},{4,12},{5,13},{6,14},{7,15},{8,16},{9,17... | collective-permute-start | bytes 1572872 | tf_op jit(solution)/shard_map/ppermute | solution.py:255
  5.7 3.2 %collective-permute-start.3 = (bf16[512,512]{1,0:T(8,128)(2,1)S(1)}, bf16[512,512]{1,0:T(8,128)(2,1)S(1)}, u32[]{:S(2)}, u32[]{:S(2)}) collective-permute-start(bf16[512,512]{1,0:T(8,128)(2,1)S(1)} %pad_maximum_fusion.5.refs_0_.refs_6_), channel_id=1, source_target_pairs={{0,8},{1,9},{2,10},{3,11},{4,12},{5,13},{6,14},{7,15},{8,16},{9,17... | collective-permute-start | bytes 1572872 | tf_op jit(solution)/shard_map/ppermute | solution.py:255
  10.4 6.7 %collective-permute-done.refs_4_.refs_10_ = bf16[512,512]{1,0:T(8,128)(2,1)S(1)} collective-permute-done((bf16[512,512]{1,0:T(8,128)(2,1)S(1)}, bf16[512,512]{1,0:T(8,128)(2,1)S(1)}, u32[]{:S(2)}, u32[]{:S(2)}) %collective-permute-start) | collective-permute-done | bytes 524320 | tf_op jit(solution)/shard_map/ppermute | solution.py:255
  17.2 1.3 collective-permute-start.8
  18.6 3.3 %collective-permute-start.1 = (bf16[512,1024]{1,0:T(8,128)(2,1)S(1)}, bf16[512,1024]{1,0:T(8,128)(2,1)S(1)}, u32[]{:S(2)}, u32[]{:S(2)}) collective-permute-start(bf16[512,1024]{1,0:T(8,128)(2,1)S(1)} %pad_maximum_fusion), channel_id=1, source_target_pairs={{0,8},{1,9},{2,10},{3,11},{4,12},{5,13},{6,14},{7,15},{8,16},{9,17... | collective-permute-start | bytes 3145736 | tf_op jit(solution)/shard_map/ppermute | solution.py:255
  21.9 6.4 %collective-permute-done.3.refs_4_.refs_10_ = bf16[512,512]{1,0:T(8,128)(2,1)S(1)} collective-permute-done((bf16[512,512]{1,0:T(8,128)(2,1)S(1)}, bf16[512,512]{1,0:T(8,128)(2,1)S(1)}, u32[]{:S(2)}, u32[]{:S(2)}) %collective-permute-start.3) | collective-permute-done | bytes 524320 | tf_op jit(solution)/shard_map/ppermute | solution.py:255
  28.4 1.3 collective-permute-start.4
  30.9 3.2 %collective-permute-start.7 = (bf16[512,1024]{1,0:T(8,128)(2,1)}, bf16[512,1024]{1,0:T(8,128)(2,1)S(1)}, u32[]{:S(2)}, u32[]{:S(2)}) collective-permute-start(bf16[512,1024]{1,0:T(8,128)(2,1)} %pad_maximum_fusion.1), channel_id=1, source_target_pairs={{0,8},{1,9},{2,10},{3,11},{4,12},{5,13},{6,14},{7,15},{8,16},{9,17... | collective-permute-start | bytes 3145736 | tf_op jit(solution)/shard_map/ppermute | solution.py:255
  34.2 1.3 collective-permute-start.10
  35.5 3.6 %collective-permute-start.9 = (bf16[512,512]{1,0:T(8,128)(2,1)S(1)}, bf16[512,512]{1,0:T(8,128)(2,1)S(1)}, u32[]{:S(2)}, u32[]{:S(2)}) collective-permute-start(bf16[512,512]{1,0:T(8,128)(2,1)S(1)} %get-tuple-element.23), channel_id=1, source_target_pairs={{0,1},{1,2},{2,3},{3,0},{4,5},{5,6},{6,7},{7,4},{8,9},{9,10},{10,1... | collective-permute-start | bytes 1572872 | tf_op jit(solution)/shard_map/ppermute | solution.py:270
  39.2 1.2 broadcast_select_fusion.10
  40.4 4.7 %collective-permute-start.5 = (bf16[512,512]{1,0:T(8,128)(2,1)}, bf16[512,512]{1,0:T(8,128)(2,1)}, u32[]{:S(2)}, u32[]{:S(2)}) collective-permute-start(bf16[512,512]{1,0:T(8,128)(2,1)} %get-tuple-element.21), channel_id=1, source_target_pairs={{0,1},{1,2},{2,3},{3,0},{4,5},{5,6},{6,7},{7,4},{8,9},{9,10},{10,1... | collective-permute-start | bytes 1572872 | tf_op jit(solution)/shard_map/ppermute | solution.py:270
  45.1 5.7 %collective-permute-done.1.refs_5_.refs_11_.refs_4_.refs_10_ = bf16[512,1024]{1,0:T(8,128)(2,1)S(1)} collective-permute-done((bf16[512,1024]{1,0:T(8,128)(2,1)S(1)}, bf16[512,1024]{1,0:T(8,128)(2,1)S(1)}, u32[]{:S(2)}, u32[]{:S(2)}) %collective-permute-start.1) | collective-permute-done | bytes 1048608 | tf_op jit(solution)/shard_map/ppermute | solution.py:255
  50.8 1.2 collective-permute-start.6
  53.2 1.2 collective-permute-start.15
  54.4 24.4 %shard_map.55 = (bf16[512,8192]{1,0:T(8,128)(2,1)}, s32[1]{0:T(128)}) custom-call(s32[1]{0:T(128)} %bitcast.place_ref, s32[56]{0:T(128)S(1)} %pad_add_fusion.table_ref, bf16[512,8192]{1,0:T(8,128)(2,1)} %q_ref.7, bf16[512,512]{1,0:T(8,128)(2,1)S(1)} %copy-done.5, bf16[512,512]{1,0:T(8,128)(2,1)S(1)} %collective-permute-done.9.refs_1_.refs_7_, ...), custom_call_target="tpu_custom_call" | custom-call | flops 5000000000 | bytes 1 | tf_op jit(solution)/shard_map/pallas_call | solution.py:199
  79.9 3.3 %collective-permute-start.2 = (bf16[512,512]{1,0:T(8,128)(2,1)}, bf16[512,512]{1,0:T(8,128)(2,1)}, u32[]{:S(2)}, u32[]{:S(2)}) collective-permute-start(bf16[512,512]{1,0:T(8,128)(2,1)} %get-tuple-element.26), channel_id=1, source_target_pairs={{0,8},{1,9},{2,10},{3,11},{4,12},{5,13},{6,14},{7,15},{8,16},{9,17... | collective-permute-start | bytes 1572872 | tf_op jit(solution)/shard_map/ppermute | solution.py:255
  84.6 1.1 broadcast_select_fusion.7
  85.7 5.0 %collective-permute-start.16 = (bf16[512,512]{1,0:T(8,128)(2,1)}, bf16[512,512]{1,0:T(8,128)(2,1)}, u32[]{:S(2)}, u32[]{:S(2)}) collective-permute-start(bf16[512,512]{1,0:T(8,128)(2,1)} %get-tuple-element.17), channel_id=1, source_target_pairs={{0,1},{1,2},{2,3},{3,0},{4,5},{5,6},{6,7},{7,4},{8,9},{9,10},{10,1... | collective-permute-start | bytes 1572872 | tf_op jit(solution)/shard_map/ppermute | solution.py:270
  90.9 24.5 %shard_map.56 = (bf16[512,8192]{1,0:T(8,128)(2,1)}, s32[1]{0:T(128)}) custom-call(s32[1]{0:T(128)} %bitcast.place_ref, s32[56]{0:T(128)S(1)} %pad_add_fusion.table_ref, bf16[512,8192]{1,0:T(8,128)(2,1)} %q_ref.7, bf16[512,512]{1,0:T(8,128)(2,1)S(1)} %pad_maximum_fusion.5.refs_0_.refs_6_, ...), custom_call_target="tpu_custom_call", output_to_operand_aliasing={{0}: (15, {})} | custom-call | flops 5000000000 | bytes 1 | tf_op jit(solution)/shard_map/pallas_call | solution.py:199
  116.1 3.2 %collective-permute-start.14 = (bf16[512,512]{1,0:T(8,128)(2,1)}, bf16[512,512]{1,0:T(8,128)(2,1)S(1)}, u32[]{:S(2)}, u32[]{:S(2)}) collective-permute-start(bf16[512,512]{1,0:T(8,128)(2,1)} %get-tuple-element.27), channel_id=1, source_target_pairs={{0,8},{1,9},{2,10},{3,11},{4,12},{5,13},{6,14},{7,15},{8,16},{9,17... | collective-permute-start | bytes 1572872 | tf_op jit(solution)/shard_map/ppermute | solution.py:255
  122.7 24.6 %shard_map.57 = (bf16[512,8192]{1,0:T(8,128)(2,1)}, s32[1]{0:T(128)}) custom-call(s32[1]{0:T(128)} %bitcast.place_ref, s32[56]{0:T(128)S(1)} %pad_add_fusion.table_ref, bf16[512,8192]{1,0:T(8,128)(2,1)} %q_ref.7, bf16[512,512]{1,0:T(8,128)(2,1)S(1)} %pad_maximum_fusion.3.refs_0_.refs_6_, ...), custom_call_target="tpu_custom_call", output_to_operand_aliasing={{0}: (15, {})} | custom-call | flops 5000000000 | bytes 1 | tf_op jit(solution)/shard_map/pallas_call | solution.py:199
  147.3 24.5 %shard_map.58 = (bf16[512,8192]{1,0:T(8,128)(2,1)}, s32[1]{0:T(128)}) custom-call(s32[1]{0:T(128)} %bitcast.place_ref, s32[56]{0:T(128)S(1)} %pad_add_fusion.table_ref, bf16[512,8192]{1,0:T(8,128)(2,1)} %q_ref.7, bf16[512,512]{1,0:T(8,128)(2,1)S(1)} %pad_maximum_fusion.2.refs_0_.refs_6_, ...), custom_call_target="tpu_custom_call", output_to_operand_aliasing={{0}: (15, {})} | custom-call | flops 5000000000 | bytes 1 | tf_op jit(solution)/shard_map/pallas_call | solution.py:199
  (57 shorter events, 9.1 us)
Async XLA Ops:
  2.4 14.8 %copy-start.4 = (bf16[512,512]{1,0:T(8,128)(2,1)}, bf16[512,512]{1,0:T(8,128)(2,1)S(1)}, u32[]{:S(2)}) copy-start(bf16[512,512]{1,0:T(8,128)(2,1)S(1)} %pad_maximum_fusion.4.refs_0_.refs_6_) | copy-start | bytes 1572868
  2.4 14.7 %collective-permute-start = (bf16[512,512]{1,0:T(8,128)(2,1)S(1)}, bf16[512,512]{1,0:T(8,128)(2,1)S(1)}, u32[]{:S(2)}, u32[]{:S(2)}) collective-permute-start(bf16[512,512]{1,0:T(8,128)(2,1)S(1)} %pad_maximum_fusion.4.refs_0_.refs_6_), channel_id=1, source_target_pairs={{0,8},{1,9},{2,10},{3,11},{4,12},{5,13},{6,14},{7,15},{8,16},{9,17... | collective-permute-start | bytes 1572872 | tf_op jit(solution)/shard_map/ppermute | solution.py:255
  5.7 22.7 %collective-permute-start.3 = (bf16[512,512]{1,0:T(8,128)(2,1)S(1)}, bf16[512,512]{1,0:T(8,128)(2,1)S(1)}, u32[]{:S(2)}, u32[]{:S(2)}) collective-permute-start(bf16[512,512]{1,0:T(8,128)(2,1)S(1)} %pad_maximum_fusion.5.refs_0_.refs_6_), channel_id=1, source_target_pairs={{0,8},{1,9},{2,10},{3,11},{4,12},{5,13},{6,14},{7,15},{8,16},{9,17... | collective-permute-start | bytes 1572872 | tf_op jit(solution)/shard_map/ppermute | solution.py:255
  17.1 11.3 %copy-start.6 = (bf16[512,512]{1,0:T(8,128)(2,1)}, bf16[512,512]{1,0:T(8,128)(2,1)S(1)}, u32[]{:S(2)}) copy-start(bf16[512,512]{1,0:T(8,128)(2,1)S(1)} %collective-permute-done.refs_4_.refs_10_) | copy-start | bytes 1572868
  17.2 16.9 %collective-permute-start.8 = (bf16[512,512]{1,0:T(8,128)(2,1)S(1)}, bf16[512,512]{1,0:T(8,128)(2,1)S(1)}, u32[]{:S(2)}, u32[]{:S(2)}) collective-permute-start(bf16[512,512]{1,0:T(8,128)(2,1)S(1)} %broadcast_select_fusion.3), channel_id=1, source_target_pairs={{0,4},{1,5},{2,6},{3,7},{4,0},{5,1},{6,2},{7,3},{8,12},{9,13},{10,... | collective-permute-start | bytes 1572872 | tf_op jit(solution)/shard_map/ppermute | solution.py:266
  18.6 15.5 %copy-start.5 = (bf16[512,512]{1,0:T(8,128)(2,1)S(1)}, bf16[512,512]{1,0:T(8,128)(2,1)}, u32[]{:S(2)}) copy-start(bf16[512,512]{1,0:T(8,128)(2,1)} %copy-done.4) | copy-start | bytes 1572868
  18.6 32.2 %collective-permute-start.1 = (bf16[512,1024]{1,0:T(8,128)(2,1)S(1)}, bf16[512,1024]{1,0:T(8,128)(2,1)S(1)}, u32[]{:S(2)}, u32[]{:S(2)}) collective-permute-start(bf16[512,1024]{1,0:T(8,128)(2,1)S(1)} %pad_maximum_fusion), channel_id=1, source_target_pairs={{0,8},{1,9},{2,10},{3,11},{4,12},{5,13},{6,14},{7,15},{8,16},{9,17... | collective-permute-start | bytes 3145736 | tf_op jit(solution)/shard_map/ppermute | solution.py:255
  28.4 10.8 %collective-permute-start.4 = (bf16[512,512]{1,0:T(8,128)(2,1)S(1)}, bf16[512,512]{1,0:T(8,128)(2,1)S(1)}, u32[]{:S(2)}, u32[]{:S(2)}) collective-permute-start(bf16[512,512]{1,0:T(8,128)(2,1)S(1)} %broadcast_select_fusion.4), channel_id=1, source_target_pairs={{0,4},{1,5},{2,6},{3,7},{4,0},{5,1},{6,2},{7,3},{8,12},{9,13},{10,... | collective-permute-start | bytes 1572872 | tf_op jit(solution)/shard_map/ppermute | solution.py:266
  30.9 52.4 %collective-permute-start.7 = (bf16[512,1024]{1,0:T(8,128)(2,1)}, bf16[512,1024]{1,0:T(8,128)(2,1)S(1)}, u32[]{:S(2)}, u32[]{:S(2)}) collective-permute-start(bf16[512,1024]{1,0:T(8,128)(2,1)} %pad_maximum_fusion.1), channel_id=1, source_target_pairs={{0,8},{1,9},{2,10},{3,11},{4,12},{5,13},{6,14},{7,15},{8,16},{9,17... | collective-permute-start | bytes 3145736 | tf_op jit(solution)/shard_map/ppermute | solution.py:255
  34.2 19.0 %collective-permute-start.10 = (bf16[512,512]{1,0:T(8,128)(2,1)S(1)}, bf16[512,512]{1,0:T(8,128)(2,1)S(1)}, u32[]{:S(2)}, u32[]{:S(2)}) collective-permute-start(bf16[512,512]{1,0:T(8,128)(2,1)S(1)} %get-tuple-element.24), channel_id=1, source_target_pairs={{0,2},{1,3},{2,0},{3,1},{4,6},{5,7},{6,4},{7,5},{8,10},{9,11},{10,... | collective-permute-start | bytes 1572872 | tf_op jit(solution)/shard_map/ppermute | solution.py:266
  35.5 18.9 %copy-start.7 = (bf16[512,512]{1,0:T(8,128)(2,1)S(1)}, bf16[512,512]{1,0:T(8,128)(2,1)}, u32[]{:S(2)}) copy-start(bf16[512,512]{1,0:T(8,128)(2,1)} %copy-done.6) | copy-start | bytes 1572868
  35.5 18.9 %collective-permute-start.9 = (bf16[512,512]{1,0:T(8,128)(2,1)S(1)}, bf16[512,512]{1,0:T(8,128)(2,1)S(1)}, u32[]{:S(2)}, u32[]{:S(2)}) collective-permute-start(bf16[512,512]{1,0:T(8,128)(2,1)S(1)} %get-tuple-element.23), channel_id=1, source_target_pairs={{0,1},{1,2},{2,3},{3,0},{4,5},{5,6},{6,7},{7,4},{8,9},{9,10},{10,1... | collective-permute-start | bytes 1572872 | tf_op jit(solution)/shard_map/ppermute | solution.py:270
  39.2 14.0 %copy-start.2 = (bf16[512,512]{1,0:T(8,128)(2,1)}, bf16[512,512]{1,0:T(8,128)(2,1)S(1)}, u32[]{:S(2)}) copy-start(bf16[512,512]{1,0:T(8,128)(2,1)S(1)} %collective-permute-done.4.refs_3_.refs_9_) | copy-start | bytes 1572868
  40.4 50.3 %collective-permute-start.5 = (bf16[512,512]{1,0:T(8,128)(2,1)}, bf16[512,512]{1,0:T(8,128)(2,1)}, u32[]{:S(2)}, u32[]{:S(2)}) collective-permute-start(bf16[512,512]{1,0:T(8,128)(2,1)} %get-tuple-element.21), channel_id=1, source_target_pairs={{0,1},{1,2},{2,3},{3,0},{4,5},{5,6},{6,7},{7,4},{8,9},{9,10},{10,1... | collective-permute-start | bytes 1572872 | tf_op jit(solution)/shard_map/ppermute | solution.py:270
  50.8 28.0 %copy-start = (bf16[512,1024]{1,0:T(8,128)(2,1)}, bf16[512,1024]{1,0:T(8,128)(2,1)S(1)}, u32[]{:S(2)}) copy-start(bf16[512,1024]{1,0:T(8,128)(2,1)S(1)} %collective-permute-done.1.refs_5_.refs_11_.refs_4_.refs_10_) | copy-start | bytes 3145732
  50.8 40.1 %collective-permute-start.6 = (bf16[512,512]{1,0:T(8,128)(2,1)}, bf16[512,512]{1,0:T(8,128)(2,1)}, u32[]{:S(2)}, u32[]{:S(2)}) collective-permute-start(bf16[512,512]{1,0:T(8,128)(2,1)} %get-tuple-element.22), channel_id=1, source_target_pairs={{0,2},{1,3},{2,0},{3,1},{4,6},{5,7},{6,4},{7,5},{8,10},{9,11},{10,... | collective-permute-start | bytes 1572872 | tf_op jit(solution)/shard_map/ppermute | solution.py:266
  53.2 31.4 %collective-permute-start.15 = (bf16[512,512]{1,0:T(8,128)(2,1)}, bf16[512,512]{1,0:T(8,128)(2,1)}, u32[]{:S(2)}, u32[]{:S(2)}) collective-permute-start(bf16[512,512]{1,0:T(8,128)(2,1)} %get-tuple-element.25), channel_id=1, source_target_pairs={{0,4},{1,5},{2,6},{3,7},{4,0},{5,1},{6,2},{7,3},{8,12},{9,13},{10,... | collective-permute-start | bytes 1572872 | tf_op jit(solution)/shard_map/ppermute | solution.py:266
  79.9 39.4 %collective-permute-start.2 = (bf16[512,512]{1,0:T(8,128)(2,1)}, bf16[512,512]{1,0:T(8,128)(2,1)}, u32[]{:S(2)}, u32[]{:S(2)}) collective-permute-start(bf16[512,512]{1,0:T(8,128)(2,1)} %get-tuple-element.26), channel_id=1, source_target_pairs={{0,8},{1,9},{2,10},{3,11},{4,12},{5,13},{6,14},{7,15},{8,16},{9,17... | collective-permute-start | bytes 1572872 | tf_op jit(solution)/shard_map/ppermute | solution.py:255
  84.3 35.0 %collective-permute-start.11 = (bf16[512,512]{1,0:T(8,128)(2,1)}, bf16[512,512]{1,0:T(8,128)(2,1)}, u32[]{:S(2)}, u32[]{:S(2)}) collective-permute-start(bf16[512,512]{1,0:T(8,128)(2,1)} %get-tuple-element.28), channel_id=1, source_target_pairs={{0,4},{1,5},{2,6},{3,7},{4,0},{5,1},{6,2},{7,3},{8,12},{9,13},{10,... | collective-permute-start | bytes 1572872 | tf_op jit(solution)/shard_map/ppermute | solution.py:266
  85.7 37.0 %collective-permute-start.16 = (bf16[512,512]{1,0:T(8,128)(2,1)}, bf16[512,512]{1,0:T(8,128)(2,1)}, u32[]{:S(2)}, u32[]{:S(2)}) collective-permute-start(bf16[512,512]{1,0:T(8,128)(2,1)} %get-tuple-element.17), channel_id=1, source_target_pairs={{0,1},{1,2},{2,3},{3,0},{4,5},{5,6},{6,7},{7,4},{8,9},{9,10},{10,1... | collective-permute-start | bytes 1572872 | tf_op jit(solution)/shard_map/ppermute | solution.py:270
  90.7 32.0 %collective-permute-start.17 = (bf16[512,512]{1,0:T(8,128)(2,1)}, bf16[512,512]{1,0:T(8,128)(2,1)}, u32[]{:S(2)}, u32[]{:S(2)}) collective-permute-start(bf16[512,512]{1,0:T(8,128)(2,1)} %get-tuple-element.18), channel_id=1, source_target_pairs={{0,2},{1,3},{2,0},{3,1},{4,6},{5,7},{6,4},{7,5},{8,10},{9,11},{10,... | collective-permute-start | bytes 1572872 | tf_op jit(solution)/shard_map/ppermute | solution.py:266
  116.1 31.1 %collective-permute-start.14 = (bf16[512,512]{1,0:T(8,128)(2,1)}, bf16[512,512]{1,0:T(8,128)(2,1)S(1)}, u32[]{:S(2)}, u32[]{:S(2)}) collective-permute-start(bf16[512,512]{1,0:T(8,128)(2,1)} %get-tuple-element.27), channel_id=1, source_target_pairs={{0,8},{1,9},{2,10},{3,11},{4,12},{5,13},{6,14},{7,15},{8,16},{9,17... | collective-permute-start | bytes 1572872 | tf_op jit(solution)/shard_map/ppermute | solution.py:255
  120.5 26.8 %collective-permute-start.12 = (bf16[512,512]{1,0:T(8,128)(2,1)S(1)}, bf16[512,512]{1,0:T(8,128)(2,1)S(1)}, u32[]{:S(2)}, u32[]{:S(2)}) collective-permute-start(bf16[512,512]{1,0:T(8,128)(2,1)S(1)} %get-tuple-element.19), channel_id=1, source_target_pairs={{0,1},{1,2},{2,3},{3,0},{4,5},{5,6},{6,7},{7,4},{8,9},{9,10},{10,1... | collective-permute-start | bytes 1572872 | tf_op jit(solution)/shard_map/ppermute | solution.py:270
  121.6 25.7 %collective-permute-start.13 = (bf16[512,512]{1,0:T(8,128)(2,1)S(1)}, bf16[512,512]{1,0:T(8,128)(2,1)S(1)}, u32[]{:S(2)}, u32[]{:S(2)}) collective-permute-start(bf16[512,512]{1,0:T(8,128)(2,1)S(1)} %get-tuple-element.20), channel_id=1, source_target_pairs={{0,2},{1,3},{2,0},{3,1},{4,6},{5,7},{6,4},{7,5},{8,10},{9,11},{10,... | collective-permute-start | bytes 1572872 | tf_op jit(solution)/shard_map/ppermute | solution.py:266
  (4 other events, 31.4 us)

commit v3 on v2

--- a/solution.py
+++ b/solution.py
@@ -242,8 +242,10 @@
     held = []
     for first, heads in zip(firsts, CHUNKS):
         columns = slice(first * HEAD_SIZE, (first + heads) * HEAD_SIZE)
-        kv = jnp.concatenate([keys[:, columns], values[:, columns]], 1)
-        held.append({0: (lax.optimization_barrier(kv), 0)})
+        kv = lax.optimization_barrier(jnp.concatenate([keys[:, columns], values[:, columns]], 1))
+        held.append({0: (kv, 0)})
+        if first == 0:
+            keys, values, _ = lax.optimization_barrier((keys, values, kv))
 
     def part_of(chunk, source):
         array, column = held[chunk][source]

time: 174 us -> 174 us (level)
  starting transfers between devices: 41.8 us -> 39 us
    ppermute x8, waiting for transfers between devices: 0.07 us -> 2.94 us  [swap(): held[chunk][distance] = (lax.ppermute(sent, AXES, pairs), 0)]
    ppermute x6, waiting for transfers between devices: 18.8 us -> 16.9 us  [climb(): arrived, column = (lax.ppermute(sent, AXES, up), 0)]
    ppermute x4, starting transfers between devices: 14.4 us -> 12.6 us  [swap(): held[chunk][1] = (lax.ppermute(sent, AXES, pairs), 0)]
    slice x1 -> x3, local copies, waits for them, and re-layouts: 2.36 us -> 3.97 us  [the longest x2 3 us: body(): keys[:, columns]]
  transfers between devices with their start and end apart: 18 -> 18, of which waited for: 4 -> 5; matrix products, arithmetic and copies ran while one was open for 5% -> 6% of each run, Pallas kernels for 43% -> 43%
where the time goes in v3:
time: 174 us; the launch traced here: 172 us
  Pallas kernels  98 us (56%)
  starting transfers between devices  39 us (22%)
  waiting for transfers between devices  19.8 us (11%)
  other arithmetic  8.17 us (5%)
  local copies, waits for them, and re-layouts  4.45 us (3%)
  between operations  2.27 us (1%)
    pallas_call x4, Pallas kernels, attend_chunk(): pl.pallas_call(functools.partial(attend_kernel, levels, blocks, parts, so...  98 us
    ppermute x6, starting transfers between devices, climb(): arrived, column = (lax.ppermute(sent, AXES, up), 0)  19.6 us
    ppermute x6, waiting for transfers between devices, climb(): arrived, column = (lax.ppermute(sent, AXES, up), 0)  16.9 us
    ppermute x4, starting transfers between devices, swap(): held[chunk][1] = (lax.ppermute(sent, AXES, pairs), 0)  12.6 us
    ppermute x8, starting transfers between devices, swap(): held[chunk][distance] = (lax.ppermute(sent, AXES, pairs), 0)  6.8 us
    select_n x4, other arithmetic, swap(): sent = jnp.where(place & 1 > 0, sent, part_of(chunk, 0))  3.51 us
  transfers between devices with their start and end apart: 18, of which 5 were waited for; matrix products, arithmetic and copies ran while one was open for 6% of the time, Pallas kernels for 43%

profile of v3, /device:TPU:9, one launch (start us, length us, event | category | flops | bytes accessed | tf_op | source)
XLA Modules:
  0.0 171.8 jit_solution(10505943207789769503)
XLA Ops:
  2.1 3.3 %collective-permute-start = (bf16[512,512]{1,0:T(8,128)(2,1)S(1)}, bf16[512,512]{1,0:T(8,128)(2,1)S(1)}, u32[]{:S(2)}, u32[]{:S(2)}) collective-permute-start(bf16[512,512]{1,0:T(8,128)(2,1)S(1)} %pad_maximum_fusion.2.refs_0_.refs_6_), channel_id=1, source_target_pairs={{0,8},{1,9},{2,10},{3,11},{4,12},{5,13},{6,14},{7,15},{8,16},{9,17... | collective-permute-start | bytes 1572872 | tf_op jit(solution)/shard_map/ppermute | solution.py:257
  5.5 1.9 %fusion.1 = (bf16[512,256]{1,0:T(8,128)(2,1)S(1)}, bf16[512,256]{1,0:T(8,128)(2,1)S(1)}, bf16[512,256]{1,0:T(8,128)(2,1)S(1)}, bf16[512,256]{1,0:T(8,128)(2,1)},...) fusion(bf16[512,1024]{1,0:T(8,128)(2,1)S(1)} %copy-done.8, bf16[512,1024]{1,0:T(8,128)(2,1)} %param.7), kind=kLoop, calls=%fused_computation.22 | loop fusion | bytes 3145728 | tf_op jit(solution)/shard_map/slice | solution.py:245
  7.5 3.2 %collective-permute-start.3 = (bf16[512,512]{1,0:T(8,128)(2,1)S(1)}, bf16[512,512]{1,0:T(8,128)(2,1)S(1)}, u32[]{:S(2)}, u32[]{:S(2)}) collective-permute-start(bf16[512,512]{1,0:T(8,128)(2,1)S(1)} %pad_maximum_fusion.5.refs_0_.refs_6_), channel_id=1, source_target_pairs={{0,8},{1,9},{2,10},{3,11},{4,12},{5,13},{6,14},{7,15},{8,16},{9,17... | collective-permute-start | bytes 1572872 | tf_op jit(solution)/shard_map/ppermute | solution.py:257
  12.2 4.8 %collective-permute-done.refs_4_.refs_10_ = bf16[512,512]{1,0:T(8,128)(2,1)S(1)} collective-permute-done((bf16[512,512]{1,0:T(8,128)(2,1)S(1)}, bf16[512,512]{1,0:T(8,128)(2,1)S(1)}, u32[]{:S(2)}, u32[]{:S(2)}) %collective-permute-start) | collective-permute-done | bytes 524320 | tf_op jit(solution)/shard_map/ppermute | solution.py:257
  17.0 1.3 collective-permute-start.8
  18.4 3.3 %collective-permute-start.1 = (bf16[512,1024]{1,0:T(8,128)(2,1)S(1)}, bf16[512,1024]{1,0:T(8,128)(2,1)S(1)}, u32[]{:S(2)}, u32[]{:S(2)}) collective-permute-start(bf16[512,1024]{1,0:T(8,128)(2,1)S(1)} %pad_maximum_fusion), channel_id=1, source_target_pairs={{0,8},{1,9},{2,10},{3,11},{4,12},{5,13},{6,14},{7,15},{8,16},{9,17... | collective-permute-start | bytes 3145736 | tf_op jit(solution)/shard_map/ppermute | solution.py:257
  21.8 6.4 %collective-permute-done.3.refs_4_.refs_10_ = bf16[512,512]{1,0:T(8,128)(2,1)S(1)} collective-permute-done((bf16[512,512]{1,0:T(8,128)(2,1)S(1)}, bf16[512,512]{1,0:T(8,128)(2,1)S(1)}, u32[]{:S(2)}, u32[]{:S(2)}) %collective-permute-start.3) | collective-permute-done | bytes 524320 | tf_op jit(solution)/shard_map/ppermute | solution.py:257
  28.2 1.3 collective-permute-start.4
  30.7 3.2 %collective-permute-start.7 = (bf16[512,1024]{1,0:T(8,128)(2,1)}, bf16[512,1024]{1,0:T(8,128)(2,1)S(1)}, u32[]{:S(2)}, u32[]{:S(2)}) collective-permute-start(bf16[512,1024]{1,0:T(8,128)(2,1)} %pad_maximum_fusion.1), channel_id=1, source_target_pairs={{0,8},{1,9},{2,10},{3,11},{4,12},{5,13},{6,14},{7,15},{8,16},{9,17... | collective-permute-start | bytes 3145736 | tf_op jit(solution)/shard_map/ppermute | solution.py:257
  34.0 4.4 %collective-permute-start.9 = (bf16[512,512]{1,0:T(8,128)(2,1)S(1)}, bf16[512,512]{1,0:T(8,128)(2,1)S(1)}, u32[]{:S(2)}, u32[]{:S(2)}) collective-permute-start(bf16[512,512]{1,0:T(8,128)(2,1)S(1)} %get-tuple-element.27), channel_id=1, source_target_pairs={{0,1},{1,2},{2,3},{3,0},{4,5},{5,6},{6,7},{7,4},{8,9},{9,10},{10,1... | collective-permute-start | bytes 1572872 | tf_op jit(solution)/shard_map/ppermute | solution.py:272
  39.0 1.2 broadcast_select_fusion.10
  40.2 4.7 %collective-permute-start.5 = (bf16[512,512]{1,0:T(8,128)(2,1)}, bf16[512,512]{1,0:T(8,128)(2,1)}, u32[]{:S(2)}, u32[]{:S(2)}) collective-permute-start(bf16[512,512]{1,0:T(8,128)(2,1)} %get-tuple-element.25), channel_id=1, source_target_pairs={{0,1},{1,2},{2,3},{3,0},{4,5},{5,6},{6,7},{7,4},{8,9},{9,10},{10,1... | collective-permute-start | bytes 1572872 | tf_op jit(solution)/shard_map/ppermute | solution.py:272
  44.9 5.7 %collective-permute-done.1.refs_5_.refs_11_.refs_4_.refs_10_ = bf16[512,1024]{1,0:T(8,128)(2,1)S(1)} collective-permute-done((bf16[512,1024]{1,0:T(8,128)(2,1)S(1)}, bf16[512,1024]{1,0:T(8,128)(2,1)S(1)}, u32[]{:S(2)}, u32[]{:S(2)}) %collective-permute-start.1) | collective-permute-done | bytes 1048608 | tf_op jit(solution)/shard_map/ppermute | solution.py:257
  50.6 1.2 collective-permute-start.6
  53.0 1.2 collective-permute-start.15
  54.2 2.6 %collective-permute-done.10.refs_2_.refs_8_ = bf16[512,512]{1,0:T(8,128)(2,1)S(1)} collective-permute-done((bf16[512,512]{1,0:T(8,128)(2,1)S(1)}, bf16[512,512]{1,0:T(8,128)(2,1)S(1)}, u32[]{:S(2)}, u32[]{:S(2)}) %collective-permute-start.10) | collective-permute-done | bytes 524320 | tf_op jit(solution)/shard_map/ppermute | solution.py:268
  56.8 24.4 %shard_map.55 = (bf16[512,8192]{1,0:T(8,128)(2,1)}, s32[1]{0:T(128)}) custom-call(s32[1]{0:T(128)} %bitcast.place_ref, s32[56]{0:T(128)S(1)} %pad_add_fusion.table_ref, bf16[512,8192]{1,0:T(8,128)(2,1)} %q_ref.7, bf16[512,512]{1,0:T(8,128)(2,1)S(1)} %copy-done.5, bf16[512,512]{1,0:T(8,128)(2,1)S(1)} %collective-permute-done.9.refs_1_.refs_7_, ...), custom_call_target="tpu_custom_call" | custom-call | flops 5000000000 | bytes 1 | tf_op jit(solution)/shard_map/pallas_call | solution.py:199
  82.5 3.3 %collective-permute-start.2 = (bf16[512,512]{1,0:T(8,128)(2,1)}, bf16[512,512]{1,0:T(8,128)(2,1)}, u32[]{:S(2)}, u32[]{:S(2)}) collective-permute-start(bf16[512,512]{1,0:T(8,128)(2,1)} %get-tuple-element.30), channel_id=1, source_target_pairs={{0,8},{1,9},{2,10},{3,11},{4,12},{5,13},{6,14},{7,15},{8,16},{9,17... | collective-permute-start | bytes 1572872 | tf_op jit(solution)/shard_map/ppermute | solution.py:257
  87.1 1.1 broadcast_select_fusion.7
  88.3 2.4 %collective-permute-start.16 = (bf16[512,512]{1,0:T(8,128)(2,1)}, bf16[512,512]{1,0:T(8,128)(2,1)}, u32[]{:S(2)}, u32[]{:S(2)}) collective-permute-start(bf16[512,512]{1,0:T(8,128)(2,1)} %get-tuple-element.21), channel_id=1, source_target_pairs={{0,1},{1,2},{2,3},{3,0},{4,5},{5,6},{6,7},{7,4},{8,9},{9,10},{10,1... | collective-permute-start | bytes 1572872 | tf_op jit(solution)/shard_map/ppermute | solution.py:272
  90.9 24.5 %shard_map.56 = (bf16[512,8192]{1,0:T(8,128)(2,1)}, s32[1]{0:T(128)}) custom-call(s32[1]{0:T(128)} %bitcast.place_ref, s32[56]{0:T(128)S(1)} %pad_add_fusion.table_ref, bf16[512,8192]{1,0:T(8,128)(2,1)} %q_ref.7, bf16[512,512]{1,0:T(8,128)(2,1)S(1)} %pad_maximum_fusion.5.refs_0_.refs_6_, ...), custom_call_target="tpu_custom_call", output_to_operand_aliasing={{0}: (15, {})} | custom-call | flops 5000000000 | bytes 1 | tf_op jit(solution)/shard_map/pallas_call | solution.py:199
  116.1 3.2 %collective-permute-start.14 = (bf16[512,512]{1,0:T(8,128)(2,1)}, bf16[512,512]{1,0:T(8,128)(2,1)S(1)}, u32[]{:S(2)}, u32[]{:S(2)}) collective-permute-start(bf16[512,512]{1,0:T(8,128)(2,1)} %get-tuple-element.31), channel_id=1, source_target_pairs={{0,8},{1,9},{2,10},{3,11},{4,12},{5,13},{6,14},{7,15},{8,16},{9,17... | collective-permute-start | bytes 1572872 | tf_op jit(solution)/shard_map/ppermute | solution.py:257
  122.6 24.6 %shard_map.57 = (bf16[512,8192]{1,0:T(8,128)(2,1)}, s32[1]{0:T(128)}) custom-call(s32[1]{0:T(128)} %bitcast.place_ref, s32[56]{0:T(128)S(1)} %pad_add_fusion.table_ref, bf16[512,8192]{1,0:T(8,128)(2,1)} %q_ref.7, bf16[512,512]{1,0:T(8,128)(2,1)S(1)} %pad_maximum_fusion.4.refs_0_.refs_6_, ...), custom_call_target="tpu_custom_call", output_to_operand_aliasing={{0}: (15, {})} | custom-call | flops 5000000000 | bytes 1 | tf_op jit(solution)/shard_map/pallas_call | solution.py:199
  147.3 24.5 %shard_map.58 = (bf16[512,8192]{1,0:T(8,128)(2,1)}, s32[1]{0:T(128)}) custom-call(s32[1]{0:T(128)} %bitcast.place_ref, s32[56]{0:T(128)S(1)} %pad_add_fusion.table_ref, bf16[512,8192]{1,0:T(8,128)(2,1)} %q_ref.7, bf16[512,512]{1,0:T(8,128)(2,1)S(1)} %pad_maximum_fusion.3.refs_0_.refs_6_, ...), custom_call_target="tpu_custom_call", output_to_operand_aliasing={{0}: (15, {})} | custom-call | flops 5000000000 | bytes 1 | tf_op jit(solution)/shard_map/pallas_call | solution.py:199
  (61 shorter events, 11.6 us)
Async XLA Ops:
  2.1 14.9 %copy-start.4 = (bf16[512,512]{1,0:T(8,128)(2,1)}, bf16[512,512]{1,0:T(8,128)(2,1)S(1)}, u32[]{:S(2)}) copy-start(bf16[512,512]{1,0:T(8,128)(2,1)S(1)} %pad_maximum_fusion.2.refs_0_.refs_6_) | copy-start | bytes 1572868
  2.1 14.8 %collective-permute-start = (bf16[512,512]{1,0:T(8,128)(2,1)S(1)}, bf16[512,512]{1,0:T(8,128)(2,1)S(1)}, u32[]{:S(2)}, u32[]{:S(2)}) collective-permute-start(bf16[512,512]{1,0:T(8,128)(2,1)S(1)} %pad_maximum_fusion.2.refs_0_.refs_6_), channel_id=1, source_target_pairs={{0,8},{1,9},{2,10},{3,11},{4,12},{5,13},{6,14},{7,15},{8,16},{9,17... | collective-permute-start | bytes 1572872 | tf_op jit(solution)/shard_map/ppermute | solution.py:257
  7.5 20.7 %collective-permute-start.3 = (bf16[512,512]{1,0:T(8,128)(2,1)S(1)}, bf16[512,512]{1,0:T(8,128)(2,1)S(1)}, u32[]{:S(2)}, u32[]{:S(2)}) collective-permute-start(bf16[512,512]{1,0:T(8,128)(2,1)S(1)} %pad_maximum_fusion.5.refs_0_.refs_6_), channel_id=1, source_target_pairs={{0,8},{1,9},{2,10},{3,11},{4,12},{5,13},{6,14},{7,15},{8,16},{9,17... | collective-permute-start | bytes 1572872 | tf_op jit(solution)/shard_map/ppermute | solution.py:257
  16.9 11.3 %copy-start.6 = (bf16[512,512]{1,0:T(8,128)(2,1)}, bf16[512,512]{1,0:T(8,128)(2,1)S(1)}, u32[]{:S(2)}) copy-start(bf16[512,512]{1,0:T(8,128)(2,1)S(1)} %collective-permute-done.refs_4_.refs_10_) | copy-start | bytes 1572868
  17.0 16.9 %collective-permute-start.8 = (bf16[512,512]{1,0:T(8,128)(2,1)S(1)}, bf16[512,512]{1,0:T(8,128)(2,1)S(1)}, u32[]{:S(2)}, u32[]{:S(2)}) collective-permute-start(bf16[512,512]{1,0:T(8,128)(2,1)S(1)} %broadcast_select_fusion.3), channel_id=1, source_target_pairs={{0,4},{1,5},{2,6},{3,7},{4,0},{5,1},{6,2},{7,3},{8,12},{9,13},{10,... | collective-permute-start | bytes 1572872 | tf_op jit(solution)/shard_map/ppermute | solution.py:268
  18.4 15.5 %copy-start.5 = (bf16[512,512]{1,0:T(8,128)(2,1)S(1)}, bf16[512,512]{1,0:T(8,128)(2,1)}, u32[]{:S(2)}) copy-start(bf16[512,512]{1,0:T(8,128)(2,1)} %copy-done.4) | copy-start | bytes 1572868
  18.4 32.2 %collective-permute-start.1 = (bf16[512,1024]{1,0:T(8,128)(2,1)S(1)}, bf16[512,1024]{1,0:T(8,128)(2,1)S(1)}, u32[]{:S(2)}, u32[]{:S(2)}) collective-permute-start(bf16[512,1024]{1,0:T(8,128)(2,1)S(1)} %pad_maximum_fusion), channel_id=1, source_target_pairs={{0,8},{1,9},{2,10},{3,11},{4,12},{5,13},{6,14},{7,15},{8,16},{9,17... | collective-permute-start | bytes 3145736 | tf_op jit(solution)/shard_map/ppermute | solution.py:257
  28.2 10.8 %collective-permute-start.4 = (bf16[512,512]{1,0:T(8,128)(2,1)S(1)}, bf16[512,512]{1,0:T(8,128)(2,1)S(1)}, u32[]{:S(2)}, u32[]{:S(2)}) collective-permute-start(bf16[512,512]{1,0:T(8,128)(2,1)S(1)} %broadcast_select_fusion.4), channel_id=1, source_target_pairs={{0,4},{1,5},{2,6},{3,7},{4,0},{5,1},{6,2},{7,3},{8,12},{9,13},{10,... | collective-permute-start | bytes 1572872 | tf_op jit(solution)/shard_map/ppermute | solution.py:268
  30.7 55.1 %collective-permute-start.7 = (bf16[512,1024]{1,0:T(8,128)(2,1)}, bf16[512,1024]{1,0:T(8,128)(2,1)S(1)}, u32[]{:S(2)}, u32[]{:S(2)}) collective-permute-start(bf16[512,1024]{1,0:T(8,128)(2,1)} %pad_maximum_fusion.1), channel_id=1, source_target_pairs={{0,8},{1,9},{2,10},{3,11},{4,12},{5,13},{6,14},{7,15},{8,16},{9,17... | collective-permute-start | bytes 3145736 | tf_op jit(solution)/shard_map/ppermute | solution.py:257
  34.0 19.0 %collective-permute-start.9 = (bf16[512,512]{1,0:T(8,128)(2,1)S(1)}, bf16[512,512]{1,0:T(8,128)(2,1)S(1)}, u32[]{:S(2)}, u32[]{:S(2)}) collective-permute-start(bf16[512,512]{1,0:T(8,128)(2,1)S(1)} %get-tuple-element.27), channel_id=1, source_target_pairs={{0,1},{1,2},{2,3},{3,0},{4,5},{5,6},{6,7},{7,4},{8,9},{9,10},{10,1... | collective-permute-start | bytes 1572872 | tf_op jit(solution)/shard_map/ppermute | solution.py:272
  38.4 18.3 %copy-start.7 = (bf16[512,512]{1,0:T(8,128)(2,1)S(1)}, bf16[512,512]{1,0:T(8,128)(2,1)}, u32[]{:S(2)}) copy-start(bf16[512,512]{1,0:T(8,128)(2,1)} %copy-done.6) | copy-start | bytes 1572868
  38.5 18.3 %collective-permute-start.10 = (bf16[512,512]{1,0:T(8,128)(2,1)S(1)}, bf16[512,512]{1,0:T(8,128)(2,1)S(1)}, u32[]{:S(2)}, u32[]{:S(2)}) collective-permute-start(bf16[512,512]{1,0:T(8,128)(2,1)S(1)} %get-tuple-element.28), channel_id=1, source_target_pairs={{0,2},{1,3},{2,0},{3,1},{4,6},{5,7},{6,4},{7,5},{8,10},{9,11},{10,... | collective-permute-start | bytes 1572872 | tf_op jit(solution)/shard_map/ppermute | solution.py:268
  39.0 14.0 %copy-start.2 = (bf16[512,512]{1,0:T(8,128)(2,1)}, bf16[512,512]{1,0:T(8,128)(2,1)S(1)}, u32[]{:S(2)}) copy-start(bf16[512,512]{1,0:T(8,128)(2,1)S(1)} %collective-permute-done.4.refs_3_.refs_9_) | copy-start | bytes 1572868
  40.2 50.5 %collective-permute-start.5 = (bf16[512,512]{1,0:T(8,128)(2,1)}, bf16[512,512]{1,0:T(8,128)(2,1)}, u32[]{:S(2)}, u32[]{:S(2)}) collective-permute-start(bf16[512,512]{1,0:T(8,128)(2,1)} %get-tuple-element.25), channel_id=1, source_target_pairs={{0,1},{1,2},{2,3},{3,0},{4,5},{5,6},{6,7},{7,4},{8,9},{9,10},{10,1... | collective-permute-start | bytes 1572872 | tf_op jit(solution)/shard_map/ppermute | solution.py:272
  50.6 30.5 %copy-start = (bf16[512,1024]{1,0:T(8,128)(2,1)}, bf16[512,1024]{1,0:T(8,128)(2,1)S(1)}, u32[]{:S(2)}) copy-start(bf16[512,1024]{1,0:T(8,128)(2,1)S(1)} %collective-permute-done.1.refs_5_.refs_11_.refs_4_.refs_10_) | copy-start | bytes 3145732
  50.6 40.2 %collective-permute-start.6 = (bf16[512,512]{1,0:T(8,128)(2,1)}, bf16[512,512]{1,0:T(8,128)(2,1)}, u32[]{:S(2)}, u32[]{:S(2)}) collective-permute-start(bf16[512,512]{1,0:T(8,128)(2,1)} %get-tuple-element.26), channel_id=1, source_target_pairs={{0,2},{1,3},{2,0},{3,1},{4,6},{5,7},{6,4},{7,5},{8,10},{9,11},{10,... | collective-permute-start | bytes 1572872 | tf_op jit(solution)/shard_map/ppermute | solution.py:268
  53.0 34.2 %collective-permute-start.15 = (bf16[512,512]{1,0:T(8,128)(2,1)}, bf16[512,512]{1,0:T(8,128)(2,1)}, u32[]{:S(2)}, u32[]{:S(2)}) collective-permute-start(bf16[512,512]{1,0:T(8,128)(2,1)} %get-tuple-element.29), channel_id=1, source_target_pairs={{0,4},{1,5},{2,6},{3,7},{4,0},{5,1},{6,2},{7,3},{8,12},{9,13},{10,... | collective-permute-start | bytes 1572872 | tf_op jit(solution)/shard_map/ppermute | solution.py:268
  82.5 36.9 %collective-permute-start.2 = (bf16[512,512]{1,0:T(8,128)(2,1)}, bf16[512,512]{1,0:T(8,128)(2,1)}, u32[]{:S(2)}, u32[]{:S(2)}) collective-permute-start(bf16[512,512]{1,0:T(8,128)(2,1)} %get-tuple-element.30), channel_id=1, source_target_pairs={{0,8},{1,9},{2,10},{3,11},{4,12},{5,13},{6,14},{7,15},{8,16},{9,17... | collective-permute-start | bytes 1572872 | tf_op jit(solution)/shard_map/ppermute | solution.py:257
  86.9 32.5 %collective-permute-start.11 = (bf16[512,512]{1,0:T(8,128)(2,1)}, bf16[512,512]{1,0:T(8,128)(2,1)}, u32[]{:S(2)}, u32[]{:S(2)}) collective-permute-start(bf16[512,512]{1,0:T(8,128)(2,1)} %get-tuple-element.32), channel_id=1, source_target_pairs={{0,4},{1,5},{2,6},{3,7},{4,0},{5,1},{6,2},{7,3},{8,12},{9,13},{10,... | collective-permute-start | bytes 1572872 | tf_op jit(solution)/shard_map/ppermute | solution.py:268
  88.3 34.4 %collective-permute-start.16 = (bf16[512,512]{1,0:T(8,128)(2,1)}, bf16[512,512]{1,0:T(8,128)(2,1)}, u32[]{:S(2)}, u32[]{:S(2)}) collective-permute-start(bf16[512,512]{1,0:T(8,128)(2,1)} %get-tuple-element.21), channel_id=1, source_target_pairs={{0,1},{1,2},{2,3},{3,0},{4,5},{5,6},{6,7},{7,4},{8,9},{9,10},{10,1... | collective-permute-start | bytes 1572872 | tf_op jit(solution)/shard_map/ppermute | solution.py:272
  90.7 32.0 %collective-permute-start.17 = (bf16[512,512]{1,0:T(8,128)(2,1)}, bf16[512,512]{1,0:T(8,128)(2,1)}, u32[]{:S(2)}, u32[]{:S(2)}) collective-permute-start(bf16[512,512]{1,0:T(8,128)(2,1)} %get-tuple-element.22), channel_id=1, source_target_pairs={{0,2},{1,3},{2,0},{3,1},{4,6},{5,7},{6,4},{7,5},{8,10},{9,11},{10,... | collective-permute-start | bytes 1572872 | tf_op jit(solution)/shard_map/ppermute | solution.py:268
  116.1 31.1 %collective-permute-start.14 = (bf16[512,512]{1,0:T(8,128)(2,1)}, bf16[512,512]{1,0:T(8,128)(2,1)S(1)}, u32[]{:S(2)}, u32[]{:S(2)}) collective-permute-start(bf16[512,512]{1,0:T(8,128)(2,1)} %get-tuple-element.31), channel_id=1, source_target_pairs={{0,8},{1,9},{2,10},{3,11},{4,12},{5,13},{6,14},{7,15},{8,16},{9,17... | collective-permute-start | bytes 1572872 | tf_op jit(solution)/shard_map/ppermute | solution.py:257
  120.5 26.8 %collective-permute-start.12 = (bf16[512,512]{1,0:T(8,128)(2,1)S(1)}, bf16[512,512]{1,0:T(8,128)(2,1)S(1)}, u32[]{:S(2)}, u32[]{:S(2)}) collective-permute-start(bf16[512,512]{1,0:T(8,128)(2,1)S(1)} %get-tuple-element.23), channel_id=1, source_target_pairs={{0,1},{1,2},{2,3},{3,0},{4,5},{5,6},{6,7},{7,4},{8,9},{9,10},{10,1... | collective-permute-start | bytes 1572872 | tf_op jit(solution)/shard_map/ppermute | solution.py:272
  121.5 25.7 %collective-permute-start.13 = (bf16[512,512]{1,0:T(8,128)(2,1)S(1)}, bf16[512,512]{1,0:T(8,128)(2,1)S(1)}, u32[]{:S(2)}, u32[]{:S(2)}) collective-permute-start(bf16[512,512]{1,0:T(8,128)(2,1)S(1)} %get-tuple-element.24), channel_id=1, source_target_pairs={{0,2},{1,3},{2,0},{3,1},{4,6},{5,7},{6,4},{7,5},{8,10},{9,11},{10,... | collective-permute-start | bytes 1572872 | tf_op jit(solution)/shard_map/ppermute | solution.py:268
  (5 other events, 38.3 us)
